TPU v7x, 32 devices: a whole 2x2x4 slice. The times are simulated.
32 devices in a mesh: member: 2 (over core), space: 16 (over z, y, x).
Axes of the slice: x: 2, y: 2, z: 4, core: 2. Of those that a mesh axis runs over, the one named last changes fastest.
Arguments:
- state: float32 [64, 2, 1024, 512], P('member', None, 'space'), may hold values from -6 to 6
- courant: float32 [2, 1024, 512], P(None, 'space'), may hold values from -0.3 to 0.3
- diffusion: float32 [2, 1024, 512], P(None, 'space'), may hold values from 0.02 to 0.1
- obs_cells: int32 [8, 512], replicated, may hold values from 0 to 32767
- obs_owner: int32 [8], replicated, may hold values from 0 to 15
- batch_order: int32 [8], replicated, may hold values from 0 to 7, each once
- obs_values: float32 [8, 64, 512], replicated, may hold values from -8 to 8
- obs_error: float32 [8, 512], replicated, may hold values from 0.5 to 2
Outputs:
- analysis: float32 [64, 2, 1024, 512], P(None, None, 'space', 'member')
All inputs are finite; a program needn't handle non-finite values.
Results may differ from a plain program's by a relative error of at most 0.0003.
Values sent between devices are 32-bit elements; how exact they have to be, the bound alone decides.
No kernel may reach another device: no remote copies, remote signals or barrier semaphores. Data moves between devices by JAX's collectives and lax.ppermute only.
A program may use at most 128 MiB of HBM per device.

v0:
```python
import functools

import jax
import jax.numpy as jnp
from jax import lax
from jax.experimental import pallas as pl
from jax.experimental.pallas import tpu as pltpu
from jax.sharding import PartitionSpec as P

HIGH = lax.Precision.HIGHEST
F32 = jnp.float32
BF16 = jnp.bfloat16
LANES = 128
SUB = 8
GATHER = 32
AHEAD = 1
PACK = 8


def params(mib):
    return pltpu.CompilerParams(vmem_limit_bytes=mib * 1024 * 1024)


def unrolled(count, most):
    return max(d for d in range(1, most + 1) if count % d == 0)


def rows_loop(count, most, fn):
    step = unrolled(count, most)

    def run(i, carry):
        for u in range(step):
            fn(i * step + u)
        return carry

    lax.fori_loop(0, count // step, run, 0)


def tiled(array):
    *lead, rows, cols = array.shape
    n = len(lead)
    split = array.reshape(*lead, rows // SUB, SUB, cols // LANES, LANES)
    return jnp.transpose(split, (*range(n), n, n + 2, n + 1, n + 3))


def untiled(array):
    *lead, r8, ct, sub, lanes = array.shape
    n = len(lead)
    back = jnp.transpose(array, (*range(n), n, n + 2, n + 1, n + 3))
    return back.reshape(*lead, r8 * sub, ct * lanes)


def pack_kernel(state, flow, nu, up, down, edge_flow, edge_nu, sems):
    members, fields, r8, nct = state.shape[:4]
    sides = ((up, r8 - 1, (SUB - 2, SUB - 1)), (down, 0, (0, 1)))
    copies = []

    def copy(src, dst):
        copies.append(pltpu.make_async_copy(src, dst, sems.at[len(copies)]))

    for side, (msg, block, rows) in enumerate(sides):
        copy(flow.at[:, block], edge_flow.at[side])
        copy(nu.at[:, block], edge_nu.at[side])
    for msg, block, rows in sides:
        for field in range(fields):
            for ct in range(nct):
                for at, row in enumerate(rows):
                    copy(
                        state.at[:, field, block, ct, row, :],
                        msg.at[ct, pl.ds((field * 2 + at) * members, members), :],
                    )
    for one in copies:
        one.start()
    for one in copies[:4]:
        one.wait()
    for side, (msg, block, rows) in enumerate(sides):
        edge = (SUB - 1, 0)[side]
        for ct in range(nct):
            numbers = [edge_flow[side, k, ct, edge : edge + 1, :] for k in range(2)]
            numbers += [edge_nu[side, k, ct, edge : edge + 1, :] for k in range(fields)]
            numbers.append(jnp.zeros((PACK - 2 - fields, LANES), F32))
            msg[ct, pl.ds(2 * fields * members, PACK), :] = jnp.concatenate(numbers, axis=0)
    for one in copies[4:]:
        one.wait()


def pack_edges(state6, flow5, nu5):
    members, fields, r8, nct = state6.shape[:4]
    msg = jax.ShapeDtypeStruct((nct, 2 * fields * members + PACK, LANES), F32)
    edge = pltpu.VMEM((2, 2, nct, SUB, LANES), F32)
    return pl.pallas_call(
        pack_kernel,
        out_shape=[msg] * 2,
        in_specs=[pl.BlockSpec(memory_space=pl.ANY)] * 3,
        out_specs=[pl.BlockSpec(memory_space=pltpu.VMEM)] * 2,
        scratch_shapes=[edge, edge, pltpu.SemaphoreType.DMA((4 + 4 * fields * nct,))],
        compiler_params=params(56),
        name="pack_edges",
    )(state6, flow5, nu5)


PAD = SUB


def stencil_coefs(flow_x, flow_y, nu, col, width):
    east = nu - jnp.minimum(flow_x, 0.0)
    west = nu + jnp.maximum(flow_x, 0.0)
    north = nu - jnp.minimum(flow_y, 0.0)
    south = nu + jnp.maximum(flow_y, 0.0)
    centre = 1.0 - (east + west + north + south)
    south = jnp.where(col == 0, 0.0, south)
    north = jnp.where(col == width - 1, 0.0, north)
    return centre, west, east, south, north


def fill_coefs(coef, field, flow, nu, blocks, before=None, after=None):
    _, r8, nct = flow.shape[:3]
    width = nct * LANES
    for ct in range(nct):
        for first, count in blocks:
            shape = (count * SUB, LANES)
            col = lax.broadcasted_iota(jnp.int32, shape, 1) + ct * LANES
            part = pl.ds(first, count)
            numbers = (flow[0, part, ct], flow[1, part, ct], nu[field, part, ct])
            numbers = [x.reshape(shape) for x in numbers]
            for k, value in enumerate(stencil_coefs(*numbers, col, width)):
                coef[k, ct, pl.ds(PAD + first * SUB, count * SUB), :] = value
        for msg, row in ((before, PAD - 1), (after, PAD + r8 * SUB)):
            if msg is not None:
                col = lax.broadcasted_iota(jnp.int32, (1, LANES), 1) + ct * LANES
                base = msg.shape[1] - PACK
                numbers = [msg[ct, pl.ds(base + k, 1), :] for k in (0, 1, 2 + field)]
                for k, value in enumerate(stencil_coefs(*numbers, col, width)):
                    coef[k, ct, pl.ds(row, 1), :] = value


def stencil(mid, west, east, weights):
    nct = len(mid)
    lane = lax.broadcasted_iota(jnp.int32, (SUB, LANES), 1)
    right = [pltpu.roll(x, 1, 1) for x in mid]
    left = [pltpu.roll(x, LANES - 1, 1) for x in mid]
    out = []
    for ct in range(nct):
        south = jnp.where(lane == 0, right[(ct - 1) % nct], right[ct])
        north = jnp.where(lane == LANES - 1, left[(ct + 1) % nct], left[ct])
        centre, w_w, w_e, w_s, w_n = weights[ct]
        out.append(
            (centre * mid[ct] + w_w * west[ct]) + (w_e * east[ct] + (w_s * south + w_n * north))
        )
    return out


class Rows:
    def __init__(self, held, coef):
        self.nct, _, blocks = held.shape[-5:-2]
        self.room = blocks * SUB
        self.flat = held.reshape(held.size // LANES, LANES)
        self.coef = coef.reshape(coef.size // LANES, LANES)

    def at(self, group, ct, row):
        start = (group * self.nct + ct) * SUB * self.room + PAD + row
        return pl.ds(start, SUB, stride=self.room)

    def load(self, group, row):
        return [self.flat[self.at(group, ct, row), :] for ct in range(self.nct)]

    def weights(self, row):
        return [
            [
                self.coef[pl.ds((k * self.nct + ct) * self.room + PAD + row, SUB, stride=0), :]
                for k in range(5)
            ]
            for ct in range(self.nct)
        ]


def group_steps(group, held, between, coef, put, edges):
    groups, nct, _, blocks = held.shape[:4]
    room = blocks * SUB
    source = held.reshape(groups, nct, SUB, room, LANES)
    middle = between.reshape(nct, SUB, room, LANES)

    def block_step(block, load, store):
        at = PAD + block * SUB
        weights = [[coef[k, ct, pl.ds(at, SUB), :] for k in range(5)] for ct in range(nct)]
        for m in range(SUB):
            mid, west, east = [
                [load(ct, m, pl.ds(at + off, SUB)) for ct in range(nct)] for off in (0, -1, 1)
            ]
            for ct, value in enumerate(stencil(mid, west, east, weights)):
                store(block, ct, m, value)

    def keep(block, ct, m, value):
        middle[ct, m, pl.ds(PAD + block * SUB, SUB), :] = value

    for block in range(blocks - 2):
        block_step(block, lambda ct, m, rows: source[group, ct, m, rows, :], keep)
    if edges:
        field, inner = Rows(held, coef), Rows(between, coef)
        for row in (-1, (blocks - 2) * SUB):
            around = [field.load(group, row + off) for off in (0, -1, 1)]
            for ct, value in enumerate(stencil(*around, field.weights(row))):
                inner.flat[inner.at(0, ct, row), :] = value
    for block in range(blocks - 2):
        block_step(block, lambda ct, m, rows: middle[ct, m, rows, :], put)


def held_shape(members, nct, r8):
    return (members // SUB, nct, SUB, r8 + 2, SUB, LANES)


def cost(cells):
    return pl.CostEstimate(flops=40 * cells, bytes_accessed=8 * cells, transcendentals=0)


SMEM = pl.BlockSpec(memory_space=pltpu.SMEM)
VMEM = pl.BlockSpec(memory_space=pltpu.VMEM)


def inner_kernel(state, flow, nu, full, held0, held1, between, coef, sems):
    groups, nct, _, blocks = held0.shape[:4]
    members = groups * SUB
    r8 = blocks - 2

    def copies(field, held, group):
        return [
            pltpu.make_async_copy(
                state.at[pl.ds(group * SUB, SUB), field, :, ct],
                held.at[group, ct, :, pl.ds(1, r8)],
                sems.at[field, group, ct],
            )
            for ct in range(nct)
        ]

    for group in range(groups):
        for one in copies(0, held0, group):
            one.start()
    fill_coefs(coef, 0, flow, nu, [(0, r8)])
    flat = full.reshape(full.size // LANES, LANES)

    def run(group, carry):
        for one in copies(0, held0, group):
            one.wait()
        for one in copies(1, held1, group):
            one.start()

        def put(block, ct, m, value):
            start = (block * SUB * nct + ct) * members + group * SUB + m
            flat[pl.ds(start, SUB, stride=nct * members), :] = value

        group_steps(group, held0, between, coef, put, False)
        return carry

    lax.fori_loop(0, groups, run, 0)
    for group in range(groups):
        for one in copies(1, held1, group):
            one.wait()


def forecast_inner(state6, flow5, nu5):
    members, _, r8, nct = state6.shape[:4]
    held = held_shape(members, nct, r8)
    return pl.pallas_call(
        inner_kernel,
        out_shape=[
            jax.ShapeDtypeStruct((r8 * SUB, nct, members, LANES), F32),
            jax.ShapeDtypeStruct(held, F32),
            jax.ShapeDtypeStruct(held, F32),
        ],
        in_specs=[pl.BlockSpec(memory_space=pl.ANY)] + [VMEM] * 2,
        out_specs=[VMEM] * 3,
        scratch_shapes=[
            pltpu.VMEM(held[1:], F32),
            pltpu.VMEM((5, nct, (r8 + 2) * SUB, LANES), F32),
            pltpu.SemaphoreType.DMA((2, held[0], nct)),
        ],
        compiler_params=params(34),
        cost_estimate=cost(members * r8 * SUB * nct * LANES),
        name="forecast_inner",
    )(state6, flow5, nu5)


def edge_kernel(
    ids, cells, owner, order, flow, nu, before, after, full_in, held0_in, held1_in,
    full, held0, held1, keep, away, coef
):
    groups, nct, _, blocks = held0.shape[:4]
    members = groups * SUB
    r8 = blocks - 2
    rows = r8 * SUB
    slab, member = ids[0], ids[1]

    for field, held in ((0, held0), (1, held1)):
        view = Rows(held, coef)
        for ct in range(nct):
            for group in range(groups):
                for k in range(2):
                    part = pl.ds((2 * field + k) * members + group * SUB, SUB)
                    view.flat[view.at(group, ct, k - 2), :] = before[ct, part, :]
                    view.flat[view.at(group, ct, rows + k), :] = after[ct, part, :]

    fill_coefs(coef, 0, flow, nu, [(0, 1), (r8 - 1, 1)], before, after)
    view = Rows(held0, coef)
    for first in (0, rows - 2):
        for group in range(groups):
            old = {r: view.load(group, r) for r in range(first - 2, first + 4)}
            one = {
                r: stencil(old[r], old[r - 1], old[r + 1], view.weights(r))
                for r in range(first - 1, first + 3)
            }
            for r in range(first, first + 2):
                new = stencil(one[r], one[r - 1], one[r + 1], view.weights(r))
                for ct, value in enumerate(new):
                    full[r, ct, pl.ds(group * SUB, SUB), :] = value

    nobs = cells.shape[1]
    tiles = full.reshape(rows * nct, members, LANES)
    lane = lax.broadcasted_iota(jnp.int32, (members, LANES), 1)
    for position in range(order.shape[0]):
        batch = order[position]
        mine = owner[batch] == slab
        kept = lax.rem(position, 2) == member

        def pick(tile, carry, batch=batch, mine=mine, kept=kept, position=position):
            def some(group, acc):
                for u in range(GATHER):
                    o = group * GATHER + u
                    cell = cells[batch, tile * LANES + o]
                    tile_at = lax.shift_right_logical(cell, LANES.bit_length() - 1)
                    moved = pltpu.roll(tiles[tile_at], (o - cell) & (LANES - 1), 1)
                    acc = jnp.where(lane == o, moved, acc)
                return acc

            acc = lax.fori_loop(
                0, jnp.where(mine, LANES // GATHER, 0), some, jnp.zeros((members, LANES), F32)
            )

            @pl.when(kept)
            def _():
                keep[position // 2, tile] = acc

            @pl.when(jnp.logical_not(kept))
            def _():
                away[position // 2, tile] = acc

            return carry

        lax.fori_loop(0, nobs // LANES, pick, 0)


def forecast_edges(ids, cells, owner, order, flow5, nu5, before, after, full, held0, held1):
    members = full.shape[2]
    nct, _, blocks = held0.shape[1:4]
    nb, nobs = cells.shape
    picks = jax.ShapeDtypeStruct((nb // 2, nobs // LANES, members, LANES), F32)
    same = [jax.ShapeDtypeStruct(x.shape, F32) for x in (full, held0, held1)]
    return pl.pallas_call(
        edge_kernel,
        out_shape=[*same, picks, picks],
        in_specs=[SMEM] * 4 + [VMEM] * 7,
        out_specs=[VMEM] * 5,
        input_output_aliases={8: 0, 9: 1, 10: 2},
        scratch_shapes=[pltpu.VMEM((5, nct, blocks * SUB, LANES), F32)],
        compiler_params=params(6),
        cost_estimate=cost(members * SUB * nct * LANES),
        name="forecast_edges",
    )(ids, cells, owner, order, flow5, nu5, before, after, full, held0, held1)


def piece_kernel(group, flow, nu, before, after, held, *rest):
    full, between, coef = rest[-3:]
    rows, nct, members = full.shape[:3]
    flat = full.reshape(full.size // LANES, LANES)
    fill_coefs(coef, 1, flow, nu, [(0, rows // SUB)], before, after)

    def put(block, ct, m, value):
        start = (block * SUB * nct + ct) * members + group * SUB + m
        flat[pl.ds(start, SUB, stride=nct * members), :] = value

    group_steps(group, held, between, coef, put, True)


def forecast_piece(group, flow5, nu5, before, after, held, done):
    groups, nct, _, blocks = held.shape[:4]
    rows = (blocks - 2) * SUB
    return pl.pallas_call(
        functools.partial(piece_kernel, group),
        out_shape=jax.ShapeDtypeStruct((rows, nct, groups * SUB, LANES), F32),
        in_specs=[VMEM] * (5 + len(done)),
        out_specs=VMEM,
        input_output_aliases={5: 0} if done else {},
        scratch_shapes=[
            pltpu.VMEM(held.shape[1:], F32),
            pltpu.VMEM((5, nct, blocks * SUB, LANES), F32),
        ],
        compiler_params=params(6),
        cost_estimate=cost(SUB * rows * nct * LANES),
        name=f"forecast_members_{group}",
    )(flow5, nu5, before, after, held, *done)


def gram_kernel(ids, owner, order, keep, other, observed, variance, gh):
    slab, member = ids[0], ids[1]
    count, tiles, members = keep.shape[:3]
    for k in range(count):
        batch = order[2 * k + member]
        mine = owner[batch] == slab
        out = gh.at[k]

        @pl.when(jnp.logical_not(mine))
        def _():
            out[...] = jnp.zeros(out.shape, F32)

        @pl.when(mine)
        def _():
            pair = jnp.zeros(out.shape, F32)
            for t in range(tiles):
                a, b = keep[k, t], other[k, t]
                prior = jnp.concatenate(
                    [jnp.where(member == 0, a, b), jnp.where(member == 0, b, a)], axis=0
                )
                mean = jnp.sum(prior, axis=0, keepdims=True) / (2 * members)
                anomaly = prior - mean
                scaled = anomaly / variance[batch, :, pl.ds(t * LANES, LANES)]
                misfit = observed[batch, :, pl.ds(t * LANES, LANES)] - mean
                pair += lax.dot_general(
                    scaled,
                    jnp.concatenate([anomaly, misfit], axis=0),
                    (((1,), (1,)), ((), ())),
                    precision=HIGH,
                    preferred_element_type=F32,
                )
            h = lax.dot_general(
                pair[:, 2 * members :], rotation(2 * members), (((1,), (0,)), ((), ())),
                precision=HIGH, preferred_element_type=F32,
            )
            out[...] = jnp.concatenate([pair[:, : 2 * members], h], axis=1)


def gram(ids, owner, order, keep, other, observed, variance):
    count, _, members, _ = keep.shape
    total = 2 * members
    smem = pl.BlockSpec(memory_space=pltpu.SMEM)
    vmem = pl.BlockSpec(memory_space=pltpu.VMEM)
    return pl.pallas_call(
        gram_kernel,
        out_shape=jax.ShapeDtypeStruct((count, total, 2 * total), F32),
        in_specs=[smem] * 3 + [vmem] * 4,
        out_specs=vmem,
        compiler_params=params(12),
        name="gram",
    )(ids, owner, order, keep, other, observed, variance[:, None, :])


def rotation(size):
    step = size**-0.5
    row = lax.broadcasted_iota(jnp.int32, (size, size), 0)
    col = lax.broadcasted_iota(jnp.int32, (size, size), 1)
    v_row = (row == size - 1).astype(F32) - step
    v_col = (col == size - 1).astype(F32) - step
    return (row == col).astype(F32) - v_row * v_col / (1.0 - step)


def split3(x):
    high = x.astype(BF16)
    rest = x - high.astype(F32)
    mid = rest.astype(BF16)
    return high, mid, (rest - mid.astype(F32)).astype(BF16)


def dot32(x, y, lhs, rhs):
    parts = split3(x)
    m = x.shape[1 - lhs]
    out = None
    for k, right in enumerate(split3(y)):
        left = jnp.concatenate(parts[: 3 - k], axis=1 - lhs)
        each = lax.dot_general(
            left, right, (((lhs,), (rhs,)), ((), ())), preferred_element_type=F32
        )
        for j in reversed(range(3 - k)):
            piece = each[j * m : (j + 1) * m]
            out = piece if out is None else out + piece
    return out


def total(terms):
    while len(terms) > 1:
        terms = [x + y for x, y in zip(terms[::2], terms[1::2])]
    return terms[0]


def eliminate(a_ref, b_ref, scaled, rows_a, rows_b):
    groups = a_ref.shape[0] // SUB
    wide = (SUB, LANES)
    sub = lax.broadcasted_iota(jnp.int32, wide, 0)
    part = [pl.ds(g * SUB, SUB) for g in range(groups)]

    def column(x, k):
        return jnp.broadcast_to(x[:, k : k + 1], wide)

    def row(x, k):
        return jnp.broadcast_to(x[k : k + 1, :], wide)

    def less(x, scale, first, second, n):
        return x - scale * (first * n[0] + second * n[1])

    a_next, b_next = a_ref[part[0], :], b_ref[part[0], :]
    c = [column(a_next, k) for k in range(SUB)]
    kk, kl, ll = row(c[0], 0), row(c[1], 0), row(c[1], 1)
    for p in range(groups):
        c = [(x, x) for x in c]
        pa, pb = (a_next, a_next), (b_next, b_next)
        after = p + 1 if p + 1 < groups else None
        if after:
            a_next, b_next = a_ref[part[after], :], b_ref[part[after], :]
            e = [column(a_next, p * SUB + k) for k in range(SUB)]
        ahead = None
        for k in range(0, SUB, 2):
            (fk, ck), (fl, cl) = c[k], c[k + 1]
            scale = pl.reciprocal(kk * ll - kl * kl, approx=True)

            def pivot_rows(x, k=k, kk=kk, kl=kl, ll=ll):
                u, w = row(x, k), row(x, k + 1)
                return ll * u - kl * w, kk * w - kl * u

            def inside(x, n, k=k, ck=ck, cl=cl, scale=scale):
                rest = less(x[1], scale, ck, cl, n)
                done = jnp.where(
                    sub == k, scale * n[0], jnp.where(sub == k + 1, scale * n[1], rest)
                )
                return rest, done

            n = {j: pivot_rows(c[j][0]) for j in range(k + 2, SUB)}
            if k + 2 < SUB:
                here = (k + 2, k + 3)
                left, right = ([row(x, i) for i in here] for x in (fk, fl))
                first, second = c[k + 2][0], c[k + 3][0]
                blocks = (
                    less(row(first, k + 2), scale, left[0], right[0], n[k + 2]),
                    less(row(second, k + 2), scale, left[0], right[0], n[k + 3]),
                    less(row(second, k + 3), scale, left[1], right[1], n[k + 3]),
                )
            if ahead:
                upper, lower = ahead
                m = [pivot_rows(x) for x in upper]
                if k + 2 == SUB:
                    left, right = ([row(x, i) for i in (0, 1)] for x in (e[k], e[k + 1]))
                    blocks = (
                        less(row(lower[0], 0), scale, left[0], right[0], m[0]),
                        less(row(lower[1], 0), scale, left[0], right[0], m[1]),
                        less(row(lower[1], 1), scale, left[1], right[1], m[1]),
                    )
                upper = [less(x, scale, fk, fl, y) for x, y in zip(upper, m)]
                lower = [less(x, scale, e[k], e[k + 1], y) for x, y in zip(lower, m)]
                ahead = upper, lower
            for j in range(k + 2, SUB):
                c[j] = inside(c[j], n[j])
                if after:
                    e[j] = less(e[j], scale, e[k], e[k + 1], n[j])
            if after:
                m = pivot_rows(pa[0])
                pa = inside(pa, m)
                a_next = less(a_next, scale, e[k], e[k + 1], m)
            m = pivot_rows(pb[0])
            pb = inside(pb, m)
            if after:
                b_next = less(b_next, scale, e[k], e[k + 1], m)
                if k + 2 == SUB - 2 * AHEAD:
                    ahead = [
                        [column(x, (p + 1) * SUB + j) for j in range(SUB)] for x in (pa[0], a_next)
                    ]
            kk, kl, ll = blocks
        pa, pb = pa[1], pb[1]
        scaled[part[p], :] = pb
        if after:
            c = ahead[1]
            b_ref[part[after], :] = b_next
        if p + 2 < groups:
            here = p % 2
            rows_a[here] = pa
            rows_b[here] = pb
            ra = [rows_a[here, pl.ds(k, SUB, stride=0), :] for k in range(SUB)]
            rb = [rows_b[here, pl.ds(k, SUB, stride=0), :] for k in range(SUB)]
            for g in range(p + 2, groups):
                old = a_ref[part[g], :]
                cols = [column(old, p * SUB + k) for k in range(SUB)]
                a_ref[part[g], :] = old - total([x * y for x, y in zip(cols, ra)])
                b_ref[part[g], :] = b_ref[part[g], :] - total([x * y for x, y in zip(cols, rb)])


def chain_kernel(ids, mine, other, out, a, b, scaled, rows_a, rows_b):
    member = ids[1]
    count, size, width = mine.shape
    row = lax.broadcasted_iota(jnp.int32, (size, width), 0)
    lane = lax.broadcasted_iota(jnp.int32, (size, width), 1)
    diagonal = jnp.where(row == lane, size - 1.0, 0.0)

    def step(position, vt):
        k = lax.div(position, 2)
        gh = jnp.where(lax.rem(position, 2) == member, mine[k], other[k])
        zt = jnp.where(row == size - 1, 0.0, vt)
        s = dot32(zt[:, :size], gh, 1, 0)
        v = vt[:, :size]
        t = dot32(s[:, :size], jnp.concatenate([v, v], axis=0), 1, 1)
        a[...] = jnp.where(lane == size - 1, 0.0, t) + diagonal
        b[...] = jnp.where(lane < size, zt, s - t)
        eliminate(a, b, scaled, rows_a, rows_b)
        return vt + dot32(b[...], scaled[...], 0, 0)[size:]

    unit = rotation(size)
    start = jnp.concatenate([unit, jnp.zeros_like(unit)], axis=1)
    vt = lax.fori_loop(0, 2 * count, step, start)
    w = dot32(unit, vt[:, :size], 1, 0)
    half = size // 2
    first, second = w[:, :half], w[:, half:]
    w = jnp.concatenate(
        [jnp.where(member == 0, first, second), jnp.where(member == 0, second, first)], axis=1
    )
    high = w.astype(BF16).astype(F32)
    low = w - high
    out[...] = jnp.concatenate(
        [jnp.concatenate([high, high], axis=1), jnp.concatenate([low, jnp.zeros_like(low)], axis=1)],
        axis=0,
    )


def chain(ids, mine, other):
    size = mine.shape[1]
    rows = pltpu.VMEM((2, SUB, LANES), F32)
    square = pltpu.VMEM((size, 2 * size), F32)
    return pl.pallas_call(
        chain_kernel,
        out_shape=jax.ShapeDtypeStruct((2 * size, 2 * size), F32),
        in_specs=[SMEM] + [VMEM] * 2,
        out_specs=VMEM,
        scratch_shapes=[square, square, square, rows, rows],
        compiler_params=params(12),
        name="chain",
    )(ids, mine, other)


def apply_kernel(ids, w_ref, own0, other0, own1, other1, out, held, sems):
    size = w_ref.shape[0] // 2
    rows, nct = own0.shape[:2]
    half = nct // 2
    first_tile = ids[1] * half
    weights = w_ref[...].astype(BF16)
    flat = held.reshape(held.size // LANES, LANES)

    for field, sources in enumerate(((own0, other0), (own1, other1))):

        def copy(block, slot, field=field):
            return pltpu.make_async_copy(held.at[slot], out.at[:, field, block], sems.at[slot])

        def step(block, carry, field=field, sources=sources, copy=copy):
            slot = lax.rem(block, 2)

            @pl.when((block >= 2) if field == 0 else (block >= 0))
            def _():
                copy(block, slot).wait()

            base = slot * size * half * SUB
            for r in range(SUB):
                parts = [
                    jnp.concatenate(
                        [src[block * SUB + r, first_tile + ct] for ct in range(half)], axis=1
                    )
                    for src in sources
                ]
                high = [x.astype(BF16) for x in parts]
                low = [(x - y.astype(F32)).astype(BF16) for x, y in zip(parts, high)]
                stacked = jnp.concatenate([*high, *low], axis=0)
                result = jnp.dot(weights, stacked, preferred_element_type=F32)
                result = result[:size] + result[size:]
                for ct in range(half):
                    flat[pl.ds(base + ct * SUB + r, size, stride=half * SUB), :] = result[
                        :, ct * LANES : (ct + 1) * LANES
                    ]
            copy(block, slot).start()
            return carry

        lax.fori_loop(0, rows // SUB, step, 0)
    for slot in range(2):
        copy(0, slot).wait()


def apply(ids, weights, own0, other0, own1, other1):
    rows, nct, members, _ = own0.shape
    size = 2 * members
    half = nct // 2
    r8 = rows // SUB
    return pl.pallas_call(
        apply_kernel,
        out_shape=jax.ShapeDtypeStruct((size, 2, r8, half, SUB, LANES), F32),
        in_specs=[SMEM] + [VMEM] * 5,
        out_specs=pl.BlockSpec(memory_space=pl.ANY),
        scratch_shapes=[
            pltpu.VMEM((2, size, half, SUB, LANES), F32),
            pltpu.SemaphoreType.DMA((2,)),
        ],
        compiler_params=params(12),
        name="apply",
    )(ids, weights, own0, other0, own1, other1)


def body(state, courant, diffusion, obs_cells, obs_owner, batch_order, obs_values, obs_error):
    slab = lax.axis_index("space")
    member = lax.axis_index("member")
    space = lax.axis_size("space")
    ids = jnp.stack([slab, member]).astype(jnp.int32)
    up = [(i, i + 1) for i in range(space - 1)]
    down = [(i + 1, i) for i in range(space - 1)]
    swap = [(0, 1), (1, 0)]

    state6, flow5, nu5 = tiled(state), tiled(courant), tiled(diffusion)
    up_edge, down_edge = pack_edges(state6, flow5, nu5)
    before = lax.ppermute(up_edge, "space", up)
    after = lax.ppermute(down_edge, "space", down)
    full0, held0, held1 = forecast_inner(state6, flow5, nu5)
    full0, _, held1, keep, away = forecast_edges(
        ids, obs_cells, obs_owner, batch_order, flow5, nu5, before, after, full0, held0, held1
    )
    other = lax.ppermute(away, "member", swap)
    gh = gram(ids, obs_owner, batch_order, keep, other, obs_values, obs_error)

    groups = list(range(held1.shape[0]))
    field1 = ()
    bit = 1
    while bit < space:
        received = lax.ppermute(gh, "space", [(i, i ^ bit) for i in range(space)])
        if groups:
            held1, gh = lax.optimization_barrier((held1, gh))
            field1 = forecast_piece(groups.pop(0), flow5, nu5, before, after, held1, field1)
            received, field1 = lax.optimization_barrier((received, (field1,)))
        gh = gh + received
        bit *= 2
    for group in groups:
        field1 = (forecast_piece(group, flow5, nu5, before, after, held1, field1),)
    (full1,) = field1
    theirs = lax.ppermute(gh, "member", swap)
    full0, full1, gh, theirs = lax.optimization_barrier((full0, full1, gh, theirs))
    other0 = lax.ppermute(full0, "member", swap)
    other1 = lax.ppermute(full1, "member", swap)
    weights = chain(ids, gh, theirs)
    return untiled(apply(ids, weights, full0, other0, full1, other1))


def solution(mesh):
    placed = (
        P("member", None, "space", None),
        P(None, "space", None),
        P(None, "space", None),
        P(),
        P(),
        P(),
        P(),
        P(),
    )
    return jax.shard_map(
        body,
        mesh=mesh,
        in_specs=placed,
        out_specs=P(None, None, "space", "member"),
        check_vma=False,
    )
```

profile of v0, /device:TPU:0, one launch (start us, length us, event | category | flops | bytes accessed | tf_op | source)
XLA Modules:
  0.0 84.7 jit_solution(14483219176975100357)
XLA Ops:
  0.0 2.2 %pack_edges.1 = (f32[4,136,128]{2,1,0:T(8,128)}, f32[4,136,128]{2,1,0:T(8,128)}) custom-call(f32[32,2,8,4,8,128]{5,4,3,2,1,0:T(8,128)} %bitcast.28, f32[2,8,4,8,128]{4,3,2,1,0:T(8,128)} %bitcast.14, f32[2,8,4,8,128]{4,3,2,1,0:T(8,128)} %bitcast.21), custom_call_target="tpu_custom_call" | custom-call | tf_op jit(solution)/shard_map/pack_edges/pallas_call | solution.py:91
  2.2 4.9 %collective-permute-start = (f32[4,136,128]{2,1,0:T(8,128)}, f32[4,136,128]{2,1,0:T(8,128)S(1)}, u32[]{:S(2)}, u32[]{:S(2)}) collective-permute-start(f32[4,136,128]{2,1,0:T(8,128)} %get-tuple-element.34), channel_id=1, source_target_pairs={{0,1},{1,2},{2,3},{3,4},{4,5},{5,6},{6,7},{7,8},{8,9},{9,10},{10,1... | collective-permute-start | bytes 835592 | tf_op jit(solution)/shard_map/ppermute | solution.py:717
  7.1 1.3 %collective-permute-start.1 = (f32[4,136,128]{2,1,0:T(8,128)}, f32[4,136,128]{2,1,0:T(8,128)S(1)}, u32[]{:S(2)}, u32[]{:S(2)}) collective-permute-start(f32[4,136,128]{2,1,0:T(8,128)} %get-tuple-element.35), channel_id=1, source_target_pairs={{1,0},{2,1},{3,2},{4,3},{5,4},{6,5},{7,6},{8,7},{9,8},{10,9},{11,1... | collective-permute-start | bytes 835592 | tf_op jit(solution)/shard_map/ppermute | solution.py:718
  8.5 8.9 %forecast_inner.1 = (f32[64,4,32,128]{3,2,1,0:T(8,128)S(1)}, f32[4,4,8,10,8,128]{5,4,3,2,1,0:T(8,128)S(1)}, f32[4,4,8,10,8,128]{5,4,3,2,1,0:T(8,128)S(1)}) custom-call(f32[32,2,8,4,8,128]{5,4,3,2,1,0:T(8,128)} %bitcast.29, f32[2,8,4,8,128]{4,3,2,1,0:T(8,128)S(1)} %bitcast.15, f32[2,8,4,8,128]{4,3,2,1,0:T(8,128)S(1)} %bitcast.22), custom_call_target="tpu_custom_call" | custom-call | flops 41943040 | bytes 8388608 | tf_op jit(solution)/shard_map/forecast_inner/pallas_call | solution.py:263
  17.4 1.9 %collective-permute-done.before = f32[4,136,128]{2,1,0:T(8,128)S(1)} collective-permute-done((f32[4,136,128]{2,1,0:T(8,128)}, f32[4,136,128]{2,1,0:T(8,128)S(1)}, u32[]{:S(2)}, u32[]{:S(2)}) %collective-permute-start) | collective-permute-done | bytes 278560 | tf_op jit(solution)/shard_map/ppermute | solution.py:717
  19.3 1.8 %collective-permute-done.1.after = f32[4,136,128]{2,1,0:T(8,128)S(1)} collective-permute-done((f32[4,136,128]{2,1,0:T(8,128)}, f32[4,136,128]{2,1,0:T(8,128)S(1)}, u32[]{:S(2)}, u32[]{:S(2)}) %collective-permute-start.1) | collective-permute-done | bytes 278560 | tf_op jit(solution)/shard_map/ppermute | solution.py:718
  21.1 2.5 %forecast_edges.1 = (f32[64,4,32,128]{3,2,1,0:T(8,128)S(1)}, f32[4,4,8,10,8,128]{5,4,3,2,1,0:T(8,128)S(1)}, f32[4,4,8,10,8,128]{5,4,3,2,1,0:T(8,128)S(1)}, f32[4...) custom-call(s32[2]{0:T(128)S(1)} %pad_add_fusion.ids, ...), custom_call_target="tpu_custom_call", output_to_operand_aliasing={{0}: (8, {}), {1}: (9, {}), {2}: (10, {})} | custom-call | flops 5242880 | bytes 1048576 | tf_op jit(solution)/shard_map/forecast_edges/pallas_call | solution.py:357
  23.8 1.5 %collective-permute-done.2.other = f32[4,4,32,128]{3,2,1,0:T(8,128)S(1)} collective-permute-done((f32[4,4,32,128]{3,2,1,0:T(8,128)S(1)}, f32[4,4,32,128]{3,2,1,0:T(8,128)S(1)}, u32[]{:S(2)}, u32[]{:S(2)}) %collective-permute-start.2) | collective-permute-done | bytes 262176 | tf_op jit(solution)/shard_map/ppermute | solution.py:723
  25.3 0.8 gram.1
  26.1 4.8 %collective-permute-start.3 = (f32[4,64,128]{2,1,0:T(8,128)S(1)}, f32[4,64,128]{2,1,0:T(8,128)S(1)}, u32[]{:S(2)}, u32[]{:S(2)}) collective-permute-start(f32[4,64,128]{2,1,0:T(8,128)S(1)} %gram.1), channel_id=1, source_target_pairs={{0,1},{1,0},{2,3},{3,2},{4,5},{5,4},{6,7},{7,6},{8,9},{9,8},{10,11... | collective-permute-start | bytes 393224 | tf_op jit(solution)/shard_map/ppermute | solution.py:730
  30.8 1.9 %forecast_members_0.1.rest_0_ = f32[64,4,32,128]{3,2,1,0:T(8,128)S(1)} custom-call(f32[2,8,4,8,128]{4,3,2,1,0:T(8,128)S(1)} %bitcast.17, f32[2,8,4,8,128]{4,3,2,1,0:T(8,128)S(1)} %bitcast.24, f32[4,136,128]{2,1,0:T(8,128)S(1)} %collective-permute-done.before, f32[4,136,128]{2,1,0:T(8,128)S(1)} %collective-permute-done.1.after, ...), custom_call_target="tpu_custom_call" | custom-call | flops 10485760 | bytes 2097152 | tf_op jit(solution)/shard_map/forecast_members_0/pallas_call | solution.py:386
  32.7 2.2 %collective-permute-done.3 = f32[4,64,128]{2,1,0:T(8,128)S(1)} collective-permute-done((f32[4,64,128]{2,1,0:T(8,128)S(1)}, f32[4,64,128]{2,1,0:T(8,128)S(1)}, u32[]{:S(2)}, u32[]{:S(2)}) %collective-permute-start.3) | collective-permute-done | bytes 131104 | tf_op jit(solution)/shard_map/ppermute | solution.py:730
  35.0 1.9 %forecast_members_1.1.rest_0_ = f32[64,4,32,128]{3,2,1,0:T(8,128)S(1)} custom-call(f32[2,8,4,8,128]{4,3,2,1,0:T(8,128)S(1)} %bitcast.18, f32[2,8,4,8,128]{4,3,2,1,0:T(8,128)S(1)} %bitcast.25, f32[4,136,128]{2,1,0:T(8,128)S(1)} %collective-permute-done.before, f32[4,136,128]{2,1,0:T(8,128)S(1)} %collective-permute-done.1.after, ...), custom_call_target="tpu_custom_call", output_to_operand_aliasing={{}: (5, {})} | custom-call | flops 10485760 | bytes 2097152 | tf_op jit(solution)/shard_map/forecast_members_1/pallas_call | solution.py:386
  36.9 3.6 %collective-permute-done.4 = f32[4,64,128]{2,1,0:T(8,128)S(1)} collective-permute-done((f32[4,64,128]{2,1,0:T(8,128)S(1)}, f32[4,64,128]{2,1,0:T(8,128)S(1)}, u32[]{:S(2)}, u32[]{:S(2)}) %collective-permute-start.4) | collective-permute-done | bytes 131104 | tf_op jit(solution)/shard_map/ppermute | solution.py:730
  40.6 1.9 %forecast_members_2.1.rest_0_ = f32[64,4,32,128]{3,2,1,0:T(8,128)S(1)} custom-call(f32[2,8,4,8,128]{4,3,2,1,0:T(8,128)S(1)} %bitcast.19, f32[2,8,4,8,128]{4,3,2,1,0:T(8,128)S(1)} %bitcast.26, f32[4,136,128]{2,1,0:T(8,128)S(1)} %collective-permute-done.before, f32[4,136,128]{2,1,0:T(8,128)S(1)} %collective-permute-done.1.after, ...), custom_call_target="tpu_custom_call", output_to_operand_aliasing={{}: (5, {})} | custom-call | flops 10485760 | bytes 2097152 | tf_op jit(solution)/shard_map/forecast_members_2/pallas_call | solution.py:386
  42.5 3.1 %collective-permute-done.5 = f32[4,64,128]{2,1,0:T(8,128)S(1)} collective-permute-done((f32[4,64,128]{2,1,0:T(8,128)S(1)}, f32[4,64,128]{2,1,0:T(8,128)S(1)}, u32[]{:S(2)}, u32[]{:S(2)}) %collective-permute-start.5) | collective-permute-done | bytes 131104 | tf_op jit(solution)/shard_map/ppermute | solution.py:730
  45.6 5.5 %collective-permute-start.6 = (f32[4,64,128]{2,1,0:T(8,128)S(1)}, f32[4,64,128]{2,1,0:T(8,128)S(1)}, u32[]{:S(2)}, u32[]{:S(2)}) collective-permute-start(f32[4,64,128]{2,1,0:T(8,128)S(1)} %add.14), channel_id=1, source_target_pairs={{0,8},{1,9},{2,10},{3,11},{4,12},{5,13},{6,14},{7,15},{8,0},{9,1},... | collective-permute-start | bytes 393224 | tf_op jit(solution)/shard_map/ppermute | solution.py:730
  51.1 1.9 %forecast_members_3.1.own1 = f32[64,4,32,128]{3,2,1,0:T(8,128)S(1)} custom-call(f32[2,8,4,8,128]{4,3,2,1,0:T(8,128)S(1)} %bitcast.20, f32[2,8,4,8,128]{4,3,2,1,0:T(8,128)S(1)} %bitcast.27, f32[4,136,128]{2,1,0:T(8,128)S(1)} %collective-permute-done.before, f32[4,136,128]{2,1,0:T(8,128)S(1)} %collective-permute-done.1.after, ...), custom_call_target="tpu_custom_call", output_to_operand_aliasing={{}: (5, {})} | custom-call | flops 10485760 | bytes 2097152 | tf_op jit(solution)/shard_map/forecast_members_3/pallas_call | solution.py:386
  53.0 1.1 %collective-permute-done.6 = f32[4,64,128]{2,1,0:T(8,128)S(1)} collective-permute-done((f32[4,64,128]{2,1,0:T(8,128)S(1)}, f32[4,64,128]{2,1,0:T(8,128)S(1)}, u32[]{:S(2)}, u32[]{:S(2)}) %collective-permute-start.6) | collective-permute-done | bytes 131104 | tf_op jit(solution)/shard_map/ppermute | solution.py:730
  54.1 1.3 %collective-permute-done.7.other = f32[4,64,128]{2,1,0:T(8,128)S(1)} collective-permute-done((f32[4,64,128]{2,1,0:T(8,128)S(1)}, f32[4,64,128]{2,1,0:T(8,128)S(1)}, u32[]{:S(2)}, u32[]{:S(2)}) %collective-permute-start.7) | collective-permute-done | bytes 131104 | tf_op jit(solution)/shard_map/ppermute | solution.py:740
  55.5 0.1 collective-permute-start.8
  55.6 0.4 collective-permute-start.9
  56.0 18.6 %chain.1.w_ref = f32[128,128]{1,0:T(8,128)S(1)} custom-call(s32[2]{0:T(128)S(1)} %pad_add_fusion.ids, f32[4,64,128]{2,1,0:T(8,128)S(1)} %add.15.mine, f32[4,64,128]{2,1,0:T(8,128)S(1)} %collective-permute-done.7.other), custom_call_target="tpu_custom_call" | custom-call | tf_op jit(solution)/shard_map/chain/pallas_call | solution.py:631
  74.6 10.0 %apply.1 = f32[64,2,8,2,8,128]{5,4,3,2,1,0:T(8,128)} custom-call(s32[2]{0:T(128)S(1)} %pad_add_fusion.ids, f32[128,128]{1,0:T(8,128)S(1)} %chain.1.w_ref, f32[64,4,32,128]{3,2,1,0:T(8,128)S(1)} %get-tuple-element.61.own0, f32[64,4,32,128]{3,2,1,0:T(8,128)S(1)} %collective-permute-done.8.other0, f32[64,4,32,128]{3,2,1,0:T(8,128)S(1)} %forecast_members_3.1.own1, ...), custom_call_target="tpu_custom_call" | custom-call | tf_op jit(solution)/shard_map/apply/pallas_call | solution.py:692
  (26 shorter events, 0.5 us)
Async XLA Ops:
  0.0 8.4 %copy-start = (f32[2,64,512]{2,1,0:T(8,128)S(1)}, f32[2,64,512]{2,1,0:T(8,128)}, u32[]{:S(2)}) copy-start(f32[2,64,512]{2,1,0:T(8,128)} %param.9) | copy-start | bytes 786436
  0.0 8.4 %copy-start.1 = (f32[2,64,512]{2,1,0:T(8,128)S(1)}, f32[2,64,512]{2,1,0:T(8,128)}, u32[]{:S(2)}) copy-start(f32[2,64,512]{2,1,0:T(8,128)} %param.10) | copy-start | bytes 786436
  2.2 17.0 %collective-permute-start = (f32[4,136,128]{2,1,0:T(8,128)}, f32[4,136,128]{2,1,0:T(8,128)S(1)}, u32[]{:S(2)}, u32[]{:S(2)}) collective-permute-start(f32[4,136,128]{2,1,0:T(8,128)} %get-tuple-element.34), channel_id=1, source_target_pairs={{0,1},{1,2},{2,3},{3,4},{4,5},{5,6},{6,7},{7,8},{8,9},{9,10},{10,1... | collective-permute-start | bytes 835592 | tf_op jit(solution)/shard_map/ppermute | solution.py:717
  7.1 14.0 %collective-permute-start.1 = (f32[4,136,128]{2,1,0:T(8,128)}, f32[4,136,128]{2,1,0:T(8,128)S(1)}, u32[]{:S(2)}, u32[]{:S(2)}) collective-permute-start(f32[4,136,128]{2,1,0:T(8,128)} %get-tuple-element.35), channel_id=1, source_target_pairs={{1,0},{2,1},{3,2},{4,3},{5,4},{6,5},{7,6},{8,7},{9,8},{10,9},{11,1... | collective-permute-start | bytes 835592 | tf_op jit(solution)/shard_map/ppermute | solution.py:718
  8.4 12.7 %copy-start.3 = (s32[8,512]{1,0:T(8,128)S(1)}, s32[8,512]{1,0:T(8,128)}, u32[]{:S(2)}) copy-start(s32[8,512]{1,0:T(8,128)} %cells.1) | copy-start | bytes 49156
  8.4 12.7 %copy-start.4 = (s32[8]{0:T(128)S(1)}, s32[8]{0:T(128)}, u32[]{:S(2)}) copy-start(s32[8]{0:T(128)} %owner.3) | copy-start | bytes 100
  8.4 12.7 %copy-start.5 = (s32[8]{0:T(128)S(1)}, s32[8]{0:T(128)}, u32[]{:S(2)}) copy-start(s32[8]{0:T(128)} %order.3) | copy-start | bytes 100
  21.1 2.6 %copy-start.6 = (f32[8,512]{1,0:T(8,128)S(1)}, f32[8,512]{1,0:T(8,128)}, u32[]{:S(2)}) copy-start(f32[8,512]{1,0:T(8,128)} %param.15) | copy-start | bytes 49156
  21.1 4.1 %copy-start.2 = (f32[8,64,512]{2,1,0:T(8,128)S(1)}, f32[8,64,512]{2,1,0:T(8,128)}, u32[]{:S(2)}) copy-start(f32[8,64,512]{2,1,0:T(8,128)} %observed.1) | copy-start | bytes 3145732
  23.7 1.6 %collective-permute-start.2 = (f32[4,4,32,128]{3,2,1,0:T(8,128)S(1)}, f32[4,4,32,128]{3,2,1,0:T(8,128)S(1)}, u32[]{:S(2)}, u32[]{:S(2)}) collective-permute-start(f32[4,4,32,128]{3,2,1,0:T(8,128)S(1)} %get-tuple-element.42), channel_id=1, source_target_pairs={{0,16},{16,0},{1,17},{17,1},{2,18},{18,2},{3,19},{19,3},{4,20},{20... | collective-permute-start | bytes 786440 | tf_op jit(solution)/shard_map/ppermute | solution.py:723
  26.1 8.8 %collective-permute-start.3 = (f32[4,64,128]{2,1,0:T(8,128)S(1)}, f32[4,64,128]{2,1,0:T(8,128)S(1)}, u32[]{:S(2)}, u32[]{:S(2)}) collective-permute-start(f32[4,64,128]{2,1,0:T(8,128)S(1)} %gram.1), channel_id=1, source_target_pairs={{0,1},{1,0},{2,3},{3,2},{4,5},{5,4},{6,7},{7,6},{8,9},{9,8},{10,11... | collective-permute-start | bytes 393224 | tf_op jit(solution)/shard_map/ppermute | solution.py:730
  34.9 5.6 %collective-permute-start.4 = (f32[4,64,128]{2,1,0:T(8,128)S(1)}, f32[4,64,128]{2,1,0:T(8,128)S(1)}, u32[]{:S(2)}, u32[]{:S(2)}) collective-permute-start(f32[4,64,128]{2,1,0:T(8,128)S(1)} %add.12), channel_id=1, source_target_pairs={{0,2},{1,3},{2,0},{3,1},{4,6},{5,7},{6,4},{7,5},{8,10},{9,11},{10,... | collective-permute-start | bytes 393224 | tf_op jit(solution)/shard_map/ppermute | solution.py:730
  40.5 5.0 %collective-permute-start.5 = (f32[4,64,128]{2,1,0:T(8,128)S(1)}, f32[4,64,128]{2,1,0:T(8,128)S(1)}, u32[]{:S(2)}, u32[]{:S(2)}) collective-permute-start(f32[4,64,128]{2,1,0:T(8,128)S(1)} %add.13), channel_id=1, source_target_pairs={{0,4},{1,5},{2,6},{3,7},{4,0},{5,1},{6,2},{7,3},{8,12},{9,13},{10,... | collective-permute-start | bytes 393224 | tf_op jit(solution)/shard_map/ppermute | solution.py:730
  45.6 8.5 %collective-permute-start.6 = (f32[4,64,128]{2,1,0:T(8,128)S(1)}, f32[4,64,128]{2,1,0:T(8,128)S(1)}, u32[]{:S(2)}, u32[]{:S(2)}) collective-permute-start(f32[4,64,128]{2,1,0:T(8,128)S(1)} %add.14), channel_id=1, source_target_pairs={{0,8},{1,9},{2,10},{3,11},{4,12},{5,13},{6,14},{7,15},{8,0},{9,1},... | collective-permute-start | bytes 393224 | tf_op jit(solution)/shard_map/ppermute | solution.py:730
  54.1 1.4 %collective-permute-start.7 = (f32[4,64,128]{2,1,0:T(8,128)S(1)}, f32[4,64,128]{2,1,0:T(8,128)S(1)}, u32[]{:S(2)}, u32[]{:S(2)}) collective-permute-start(f32[4,64,128]{2,1,0:T(8,128)S(1)} %add.15.mine), channel_id=1, source_target_pairs={{0,16},{16,0},{1,17},{17,1},{2,18},{18,2},{3,19},{19,3},{4,20},{20... | collective-permute-start | bytes 393224 | tf_op jit(solution)/shard_map/ppermute | solution.py:740
  55.5 19.1 %collective-permute-start.8 = (f32[64,4,32,128]{3,2,1,0:T(8,128)S(1)}, f32[64,4,32,128]{3,2,1,0:T(8,128)S(1)}, u32[]{:S(2)}, u32[]{:S(2)}) collective-permute-start(f32[64,4,32,128]{3,2,1,0:T(8,128)S(1)} %get-tuple-element.61.own0), channel_id=1, source_target_pairs={{0,16},{16,0},{1,17},{17,1},{2,18},{18,2},{3,19},{19,3},{4,20},{20... | collective-permute-start | bytes 12582920 | tf_op jit(solution)/shard_map/ppermute | solution.py:742
  55.6 19.0 %collective-permute-start.9 = (f32[64,4,32,128]{3,2,1,0:T(8,128)S(1)}, f32[64,4,32,128]{3,2,1,0:T(8,128)S(1)}, u32[]{:S(2)}, u32[]{:S(2)}) collective-permute-start(f32[64,4,32,128]{3,2,1,0:T(8,128)S(1)} %forecast_members_3.1.own1), channel_id=1, source_target_pairs={{0,16},{16,0},{1,17},{17,1},{2,18},{18,2},{3,19},{19,3},{4,20},{20... | collective-permute-start | bytes 12582920 | tf_op jit(solution)/shard_map/ppermute | solution.py:743
where the time goes:
time: 85.6 us; the launch traced here: 84.7 us
  Pallas kernels  50.4 us (59%)
  starting transfers between devices  17.2 us (20%)
  waiting for transfers between devices  16.5 us (19%)
    pallas_call x1, Pallas kernels, chain(): pl.pallas_call(chain_kernel, out_shape=jax.ShapeDtypeStruct((2 * size, 2...  18.6 us
    ppermute x4, starting transfers between devices, body(): received = lax.ppermute(gh, 'space', [(i, i ^ bit) for i in range(space)])  10.4 us
    ppermute x4, waiting for transfers between devices, body(): received = lax.ppermute(gh, 'space', [(i, i ^ bit) for i in range(space)])  9.98 us
    pallas_call x1, Pallas kernels, apply(): pl.pallas_call(apply_kernel, out_shape=jax.ShapeDtypeStruct((size, 2, r8,...  9.96 us
    pallas_call x1, Pallas kernels, forecast_inner(): pl.pallas_call(inner_kernel, out_shape=[jax.ShapeDtypeStruct((r8 * SUB, n...  8.86 us
    pallas_call x4, Pallas kernels, forecast_piece(): pl.pallas_call(functools.partial(piece_kernel, group), out_shape=jax.Shap...  7.45 us
    ppermute x1, starting transfers between devices, body(): before = lax.ppermute(up_edge, 'space', up)  4.86 us
    pallas_call x1, Pallas kernels, forecast_edges(): pl.pallas_call(edge_kernel, out_shape=[*same, picks, picks], in_specs=[SM...  2.52 us
  transfers between devices with their start and end apart: 10, of which 8 were waited for; matrix products, arithmetic and copies ran while one was open for 0% of the time, Pallas kernels for 41%

commit v1 on v0

--- a/solution.py
+++ b/solution.py
@@ -50,38 +50,62 @@
     return back.reshape(*lead, r8 * sub, ct * lanes)
 
 
-def pack_kernel(state, flow, nu, up, down, edge_flow, edge_nu, sems):
+def pack_kernel(state, flow, nu, first, second, edge_flow, edge_nu, sems):
     members, fields, r8, nct = state.shape[:4]
-    sides = ((up, r8 - 1, (SUB - 2, SUB - 1)), (down, 0, (0, 1)))
-    copies = []
-
-    def copy(src, dst):
-        copies.append(pltpu.make_async_copy(src, dst, sems.at[len(copies)]))
-
-    for side, (msg, block, rows) in enumerate(sides):
-        copy(flow.at[:, block], edge_flow.at[side])
-        copy(nu.at[:, block], edge_nu.at[side])
-    for msg, block, rows in sides:
-        for field in range(fields):
+    even = lax.rem(lax.axis_index("space"), 2) == 0
+
+    def pack(above, below):
+        sides = ((above, r8 - 1, (SUB - 2, SUB - 1)), (below, 0, (0, 1)))
+        copies = []
+
+        def copy(src, dst):
+            copies.append(pltpu.make_async_copy(src, dst, sems.at[len(copies)]))
+
+        for side, (msg, block, rows) in enumerate(sides):
+            copy(flow.at[:, block], edge_flow.at[side])
+            copy(nu.at[:, block], edge_nu.at[side])
+        for msg, block, rows in sides:
+            for field in range(fields):
+                for ct in range(nct):
+                    for at, row in enumerate(rows):
+                        copy(
+                            state.at[:, field, block, ct, row, :],
+                            msg.at[ct, pl.ds((field * 2 + at) * members, members), :],
+                        )
+        for one in copies:
+            one.start()
+        for one in copies[:4]:
+            one.wait()
+        for side, (msg, block, rows) in enumerate(sides):
+            edge = (SUB - 1, 0)[side]
             for ct in range(nct):
-                for at, row in enumerate(rows):
-                    copy(
-                        state.at[:, field, block, ct, row, :],
-                        msg.at[ct, pl.ds((field * 2 + at) * members, members), :],
-                    )
-    for one in copies:
-        one.start()
-    for one in copies[:4]:
-        one.wait()
-    for side, (msg, block, rows) in enumerate(sides):
-        edge = (SUB - 1, 0)[side]
-        for ct in range(nct):
-            numbers = [edge_flow[side, k, ct, edge : edge + 1, :] for k in range(2)]
-            numbers += [edge_nu[side, k, ct, edge : edge + 1, :] for k in range(fields)]
-            numbers.append(jnp.zeros((PACK - 2 - fields, LANES), F32))
-            msg[ct, pl.ds(2 * fields * members, PACK), :] = jnp.concatenate(numbers, axis=0)
-    for one in copies[4:]:
-        one.wait()
+                numbers = [edge_flow[side, k, ct, edge : edge + 1, :] for k in range(2)]
+                numbers += [edge_nu[side, k, ct, edge : edge + 1, :] for k in range(fields)]
+                numbers.append(jnp.zeros((PACK - 2 - fields, LANES), F32))
+                msg[ct, pl.ds(2 * fields * members, PACK), :] = jnp.concatenate(numbers, axis=0)
+        for one in copies[4:]:
+            one.wait()
+
+    @pl.when(even)
+    def _():
+        pack(first, second)
+
+    @pl.when(jnp.logical_not(even))
+    def _():
+        pack(second, first)
+
+
+class Chosen:
+    def __init__(self, flag, yes, no):
+        self.flag, self.yes, self.no, self.shape = flag, yes, no, yes.shape
+
+    def __getitem__(self, at):
+        return jnp.where(self.flag, self.yes[at], self.no[at])
+
+
+def neighbours(slab, first, second):
+    even = lax.rem(slab, 2) == 0
+    return Chosen(even, second, first), Chosen(even, first, second)
 
 
 def pack_edges(state6, flow5, nu5):
@@ -289,6 +313,7 @@
     r8 = blocks - 2
     rows = r8 * SUB
     slab, member = ids[0], ids[1]
+    before, after = neighbours(slab, before, after)
 
     for field, held in ((0, held0), (1, held1)):
         view = Rows(held, coef)
@@ -367,10 +392,11 @@
     )(ids, cells, owner, order, flow5, nu5, before, after, full, held0, held1)
 
 
-def piece_kernel(group, flow, nu, before, after, held, *rest):
+def piece_kernel(group, ids, flow, nu, first, second, held, *rest):
     full, between, coef = rest[-3:]
     rows, nct, members = full.shape[:3]
     flat = full.reshape(full.size // LANES, LANES)
+    before, after = neighbours(ids[0], first, second)
     fill_coefs(coef, 1, flow, nu, [(0, rows // SUB)], before, after)
 
     def put(block, ct, m, value):
@@ -380,15 +406,15 @@
     group_steps(group, held, between, coef, put, True)
 
 
-def forecast_piece(group, flow5, nu5, before, after, held, done):
+def forecast_piece(group, ids, flow5, nu5, before, after, held, done):
     groups, nct, _, blocks = held.shape[:4]
     rows = (blocks - 2) * SUB
     return pl.pallas_call(
         functools.partial(piece_kernel, group),
         out_shape=jax.ShapeDtypeStruct((rows, nct, groups * SUB, LANES), F32),
-        in_specs=[VMEM] * (5 + len(done)),
+        in_specs=[SMEM] + [VMEM] * (5 + len(done)),
         out_specs=VMEM,
-        input_output_aliases={5: 0} if done else {},
+        input_output_aliases={6: 0} if done else {},
         scratch_shapes=[
             pltpu.VMEM(held.shape[1:], F32),
             pltpu.VMEM((5, nct, blocks * SUB, LANES), F32),
@@ -396,7 +422,7 @@
         compiler_params=params(6),
         cost_estimate=cost(SUB * rows * nct * LANES),
         name=f"forecast_members_{group}",
-    )(flow5, nu5, before, after, held, *done)
+    )(ids, flow5, nu5, before, after, held, *done)
 
 
 def gram_kernel(ids, owner, order, keep, other, observed, variance, gh):
@@ -708,14 +734,14 @@
     member = lax.axis_index("member")
     space = lax.axis_size("space")
     ids = jnp.stack([slab, member]).astype(jnp.int32)
-    up = [(i, i + 1) for i in range(space - 1)]
-    down = [(i + 1, i) for i in range(space - 1)]
+    pairs = [
+        [(i + d, i + 1 - d) for i in range(start, space - 1, 2) for d in (0, 1)] for start in (0, 1)
+    ]
     swap = [(0, 1), (1, 0)]
 
     state6, flow5, nu5 = tiled(state), tiled(courant), tiled(diffusion)
-    up_edge, down_edge = pack_edges(state6, flow5, nu5)
-    before = lax.ppermute(up_edge, "space", up)
-    after = lax.ppermute(down_edge, "space", down)
+    edges = pack_edges(state6, flow5, nu5)
+    before, after = (lax.ppermute(x, "space", pair) for x, pair in zip(edges, pairs))
     full0, held0, held1 = forecast_inner(state6, flow5, nu5)
     full0, _, held1, keep, away = forecast_edges(
         ids, obs_cells, obs_owner, batch_order, flow5, nu5, before, after, full0, held0, held1
@@ -730,12 +756,12 @@
         received = lax.ppermute(gh, "space", [(i, i ^ bit) for i in range(space)])
         if groups:
             held1, gh = lax.optimization_barrier((held1, gh))
-            field1 = forecast_piece(groups.pop(0), flow5, nu5, before, after, held1, field1)
+            field1 = forecast_piece(groups.pop(0), ids, flow5, nu5, before, after, held1, field1)
             received, field1 = lax.optimization_barrier((received, (field1,)))
         gh = gh + received
         bit *= 2
     for group in groups:
-        field1 = (forecast_piece(group, flow5, nu5, before, after, held1, field1),)
+        field1 = (forecast_piece(group, ids, flow5, nu5, before, after, held1, field1),)
     (full1,) = field1
     theirs = lax.ppermute(gh, "member", swap)
     full0, full1, gh, theirs = lax.optimization_barrier((full0, full1, gh, theirs))

time: 85.6 us -> 83.9 us (0.980)
  starting transfers between devices: 17.2 us -> 4.63 us
  Pallas kernels: 50.4 us -> 60.9 us
  waiting for transfers between devices: 16.5 us -> 17.8 us
    ppermute x4, starting transfers between devices: 10.4 us -> 0.29 us  [body(): received = lax.ppermute(gh, 'space', [(i, i ^ bit) for i in range(space)])]
    pallas_call x1, Pallas kernels: 2.52 us -> 8.96 us  [forecast_edges(): pl.pallas_call(edge_kernel, out_shape=[*same, picks, picks], in_specs=[SM...]
    ppermute x2, starting transfers between devices: 6.15 us -> 3.68 us  [body(): lax.ppermute(x, 'space', pair)]
    ppermute x4, waiting for transfers between devices: 9.98 us -> 12.4 us  [body(): received = lax.ppermute(gh, 'space', [(i, i ^ bit) for i in range(space)])]
    pallas_call x4, Pallas kernels: 7.45 us -> 9.6 us  [forecast_piece(): pl.pallas_call(functools.partial(piece_kernel, group), out_shape=jax.Shap...]
    pallas_call x1, Pallas kernels: 0.79 us -> 2.69 us  [gram(): pl.pallas_call(gram_kernel, out_shape=jax.ShapeDtypeStruct((count, total,...]
    ppermute x2, waiting for transfers between devices: 3.7 us -> 2.52 us  [body(): lax.ppermute(x, 'space', pair)]
  transfers between devices with their start and end apart: 10 -> 10, of which waited for: 8 -> 7; matrix products, arithmetic and copies ran while one was open for 0% -> 0% of each run, Pallas kernels for 41% -> 44%
where the time goes in v1:
time: 83.9 us
  Pallas kernels  60.9 us (73%)
  waiting for transfers between devices  17.8 us (21%)
  starting transfers between devices  4.63 us (6%)
    pallas_call x1, Pallas kernels, chain(): pl.pallas_call(chain_kernel, out_shape=jax.ShapeDtypeStruct((2 * size, 2...  18.6 us
    ppermute x4, waiting for transfers between devices, body(): received = lax.ppermute(gh, 'space', [(i, i ^ bit) for i in range(space)])  12.4 us
    pallas_call x1, Pallas kernels, apply(): pl.pallas_call(apply_kernel, out_shape=jax.ShapeDtypeStruct((size, 2, r8,...  9.96 us
    pallas_call x4, Pallas kernels, forecast_piece(): pl.pallas_call(functools.partial(piece_kernel, group), out_shape=jax.Shap...  9.6 us
    pallas_call x1, Pallas kernels, forecast_edges(): pl.pallas_call(edge_kernel, out_shape=[*same, picks, picks], in_specs=[SM...  8.96 us
    pallas_call x1, Pallas kernels, forecast_inner(): pl.pallas_call(inner_kernel, out_shape=[jax.ShapeDtypeStruct((r8 * SUB, n...  8.86 us
    ppermute x2, starting transfers between devices, body(): lax.ppermute(x, 'space', pair)  3.68 us
    pallas_call x1, Pallas kernels, gram(): pl.pallas_call(gram_kernel, out_shape=jax.ShapeDtypeStruct((count, total,...  2.69 us
  transfers between devices with their start and end apart: 10, of which 7 were waited for; matrix products, arithmetic and copies ran while one was open for 0% of the time, Pallas kernels for 44%

profile of v1, /device:TPU:0, one launch (start us, length us, event | category | flops | bytes accessed | tf_op | source)
XLA Modules:
  0.0 83.9 jit_solution(11784204283365070087)
XLA Ops:
  0.0 2.2 %pack_edges.1 = (f32[4,136,128]{2,1,0:T(8,128)}, f32[4,136,128]{2,1,0:T(8,128)}) custom-call(f32[32,2,8,4,8,128]{5,4,3,2,1,0:T(8,128)} %bitcast.28, f32[2,8,4,8,128]{4,3,2,1,0:T(8,128)} %bitcast.14, f32[2,8,4,8,128]{4,3,2,1,0:T(8,128)} %bitcast.21), custom_call_target="tpu_custom_call" | custom-call | tf_op jit(solution)/shard_map/pack_edges/pallas_call | solution.py:115
  2.2 3.0 %collective-permute-start = (f32[4,136,128]{2,1,0:T(8,128)}, f32[4,136,128]{2,1,0:T(8,128)S(1)}, u32[]{:S(2)}, u32[]{:S(2)}) collective-permute-start(f32[4,136,128]{2,1,0:T(8,128)} %get-tuple-element.34), channel_id=1, source_target_pairs={{0,1},{1,0},{2,3},{3,2},{4,5},{5,4},{6,7},{7,6},{8,9},{9,8},{10,11... | collective-permute-start | bytes 835592 | tf_op jit(solution)/shard_map/ppermute | solution.py:744
  5.2 0.7 collective-permute-start.1
  6.0 8.9 %forecast_inner.1 = (f32[64,4,32,128]{3,2,1,0:T(8,128)S(1)}, f32[4,4,8,10,8,128]{5,4,3,2,1,0:T(8,128)S(1)}, f32[4,4,8,10,8,128]{5,4,3,2,1,0:T(8,128)S(1)}) custom-call(f32[32,2,8,4,8,128]{5,4,3,2,1,0:T(8,128)} %bitcast.29, f32[2,8,4,8,128]{4,3,2,1,0:T(8,128)S(1)} %bitcast.15, f32[2,8,4,8,128]{4,3,2,1,0:T(8,128)S(1)} %bitcast.22), custom_call_target="tpu_custom_call" | custom-call | flops 41943040 | bytes 8388608 | tf_op jit(solution)/shard_map/forecast_inner/pallas_call | solution.py:287
  14.8 0.1 pad_add_fusion.ids
  14.9 2.5 %collective-permute-done.before.first = f32[4,136,128]{2,1,0:T(8,128)S(1)} collective-permute-done((f32[4,136,128]{2,1,0:T(8,128)}, f32[4,136,128]{2,1,0:T(8,128)S(1)}, u32[]{:S(2)}, u32[]{:S(2)}) %collective-permute-start) | collective-permute-done | bytes 278560 | tf_op jit(solution)/shard_map/ppermute | solution.py:744
  17.5 9.0 %forecast_edges.1 = (f32[64,4,32,128]{3,2,1,0:T(8,128)S(1)}, f32[4,4,8,10,8,128]{5,4,3,2,1,0:T(8,128)S(1)}, f32[4,4,8,10,8,128]{5,4,3,2,1,0:T(8,128)S(1)}, f32[4...) custom-call(s32[2]{0:T(128)S(1)} %pad_add_fusion.ids, ...), custom_call_target="tpu_custom_call", output_to_operand_aliasing={{0}: (8, {}), {1}: (9, {}), {2}: (10, {})} | custom-call | flops 5242880 | bytes 1048576 | tf_op jit(solution)/shard_map/forecast_edges/pallas_call | solution.py:382
  26.6 1.5 %collective-permute-done.2.other = f32[4,4,32,128]{3,2,1,0:T(8,128)S(1)} collective-permute-done((f32[4,4,32,128]{3,2,1,0:T(8,128)S(1)}, f32[4,4,32,128]{3,2,1,0:T(8,128)S(1)}, u32[]{:S(2)}, u32[]{:S(2)}) %collective-permute-start.2) | collective-permute-done | bytes 262176 | tf_op jit(solution)/shard_map/ppermute | solution.py:749
  28.1 2.7 %gram.1 = f32[4,64,128]{2,1,0:T(8,128)S(1)} custom-call(s32[2]{0:T(128)S(1)} %pad_add_fusion.ids, s32[8]{0:T(128)S(1)} %copy-done.4, s32[8]{0:T(128)S(1)} %copy-done.5, f32[4,4,32,128]{3,2,1,0:T(8,128)S(1)} %get-tuple-element.41.keep, f32[4,4,32,128]{3,2,1,0:T(8,128)S(1)} %collective-permute-done.2.other, f32[8,64,512]{2,1,0:T(8,128)S(1)} %copy-done.2, ...), custom_call_target="tpu_custom_call" | custom-call | tf_op jit(solution)/shard_map/gram/pallas_call | solution.py:471
  30.8 2.4 %forecast_members_0.1.rest_0_ = f32[64,4,32,128]{3,2,1,0:T(8,128)S(1)} custom-call(s32[2]{0:T(128)S(1)} %pad_add_fusion.ids, f32[2,8,4,8,128]{4,3,2,1,0:T(8,128)S(1)} %bitcast.17, f32[2,8,4,8,128]{4,3,2,1,0:T(8,128)S(1)} %bitcast.24, f32[4,136,128]{2,1,0:T(8,128)S(1)} %collective-permute-done.before.first, ...), custom_call_target="tpu_custom_call" | custom-call | flops 10485760 | bytes 2097152 | tf_op jit(solution)/shard_map/forecast_members_0/pallas_call | solution.py:412
  33.2 2.5 %collective-permute-done.3 = f32[4,64,128]{2,1,0:T(8,128)S(1)} collective-permute-done((f32[4,64,128]{2,1,0:T(8,128)S(1)}, f32[4,64,128]{2,1,0:T(8,128)S(1)}, u32[]{:S(2)}, u32[]{:S(2)}) %collective-permute-start.3) | collective-permute-done | bytes 131104 | tf_op jit(solution)/shard_map/ppermute | solution.py:756
  35.8 0.1 collective-permute-start.4
  35.9 2.4 %forecast_members_1.1.rest_0_ = f32[64,4,32,128]{3,2,1,0:T(8,128)S(1)} custom-call(s32[2]{0:T(128)S(1)} %pad_add_fusion.ids, f32[2,8,4,8,128]{4,3,2,1,0:T(8,128)S(1)} %bitcast.18, f32[2,8,4,8,128]{4,3,2,1,0:T(8,128)S(1)} %bitcast.25, f32[4,136,128]{2,1,0:T(8,128)S(1)} %collective-permute-done.before.first, ...), custom_call_target="tpu_custom_call", output_to_operand_aliasing={{}: (6, {})} | custom-call | flops 10485760 | bytes 2097152 | tf_op jit(solution)/shard_map/forecast_members_1/pallas_call | solution.py:412
  38.3 2.5 %collective-permute-done.4 = f32[4,64,128]{2,1,0:T(8,128)S(1)} collective-permute-done((f32[4,64,128]{2,1,0:T(8,128)S(1)}, f32[4,64,128]{2,1,0:T(8,128)S(1)}, u32[]{:S(2)}, u32[]{:S(2)}) %collective-permute-start.4) | collective-permute-done | bytes 131104 | tf_op jit(solution)/shard_map/ppermute | solution.py:756
  40.9 2.4 %forecast_members_2.1.rest_0_ = f32[64,4,32,128]{3,2,1,0:T(8,128)S(1)} custom-call(s32[2]{0:T(128)S(1)} %pad_add_fusion.ids, f32[2,8,4,8,128]{4,3,2,1,0:T(8,128)S(1)} %bitcast.19, f32[2,8,4,8,128]{4,3,2,1,0:T(8,128)S(1)} %bitcast.26, f32[4,136,128]{2,1,0:T(8,128)S(1)} %collective-permute-done.before.first, ...), custom_call_target="tpu_custom_call", output_to_operand_aliasing={{}: (6, {})} | custom-call | flops 10485760 | bytes 2097152 | tf_op jit(solution)/shard_map/forecast_members_2/pallas_call | solution.py:412
  43.3 3.5 %collective-permute-done.5 = f32[4,64,128]{2,1,0:T(8,128)S(1)} collective-permute-done((f32[4,64,128]{2,1,0:T(8,128)S(1)}, f32[4,64,128]{2,1,0:T(8,128)S(1)}, u32[]{:S(2)}, u32[]{:S(2)}) %collective-permute-start.5) | collective-permute-done | bytes 131104 | tf_op jit(solution)/shard_map/ppermute | solution.py:756
  46.8 0.1 collective-permute-start.6
  46.9 2.4 %forecast_members_3.1.own1 = f32[64,4,32,128]{3,2,1,0:T(8,128)S(1)} custom-call(s32[2]{0:T(128)S(1)} %pad_add_fusion.ids, f32[2,8,4,8,128]{4,3,2,1,0:T(8,128)S(1)} %bitcast.20, f32[2,8,4,8,128]{4,3,2,1,0:T(8,128)S(1)} %bitcast.27, f32[4,136,128]{2,1,0:T(8,128)S(1)} %collective-permute-done.before.first, ...), custom_call_target="tpu_custom_call", output_to_operand_aliasing={{}: (6, {})} | custom-call | flops 10485760 | bytes 2097152 | tf_op jit(solution)/shard_map/forecast_members_3/pallas_call | solution.py:412
  49.3 3.9 %collective-permute-done.6 = f32[4,64,128]{2,1,0:T(8,128)S(1)} collective-permute-done((f32[4,64,128]{2,1,0:T(8,128)S(1)}, f32[4,64,128]{2,1,0:T(8,128)S(1)}, u32[]{:S(2)}, u32[]{:S(2)}) %collective-permute-start.6) | collective-permute-done | bytes 131104 | tf_op jit(solution)/shard_map/ppermute | solution.py:756
  53.3 1.3 %collective-permute-done.7.other = f32[4,64,128]{2,1,0:T(8,128)S(1)} collective-permute-done((f32[4,64,128]{2,1,0:T(8,128)S(1)}, f32[4,64,128]{2,1,0:T(8,128)S(1)}, u32[]{:S(2)}, u32[]{:S(2)}) %collective-permute-start.7) | collective-permute-done | bytes 131104 | tf_op jit(solution)/shard_map/ppermute | solution.py:766
  54.6 0.1 collective-permute-start.8
  54.8 0.4 collective-permute-start.9
  55.1 18.6 %chain.1.w_ref = f32[128,128]{1,0:T(8,128)S(1)} custom-call(s32[2]{0:T(128)S(1)} %pad_add_fusion.ids, f32[4,64,128]{2,1,0:T(8,128)S(1)} %add.15.mine, f32[4,64,128]{2,1,0:T(8,128)S(1)} %collective-permute-done.7.other), custom_call_target="tpu_custom_call" | custom-call | tf_op jit(solution)/shard_map/chain/pallas_call | solution.py:657
  73.7 10.0 %apply.1 = f32[64,2,8,2,8,128]{5,4,3,2,1,0:T(8,128)} custom-call(s32[2]{0:T(128)S(1)} %pad_add_fusion.ids, f32[128,128]{1,0:T(8,128)S(1)} %chain.1.w_ref, f32[64,4,32,128]{3,2,1,0:T(8,128)S(1)} %get-tuple-element.61.own0, f32[64,4,32,128]{3,2,1,0:T(8,128)S(1)} %collective-permute-done.8.other0, f32[64,4,32,128]{3,2,1,0:T(8,128)S(1)} %forecast_members_3.1.own1, ...), custom_call_target="tpu_custom_call" | custom-call | tf_op jit(solution)/shard_map/apply/pallas_call | solution.py:718
  (26 shorter events, 0.4 us)
Async XLA Ops:
  0.0 5.9 %copy-start = (f32[2,64,512]{2,1,0:T(8,128)S(1)}, f32[2,64,512]{2,1,0:T(8,128)}, u32[]{:S(2)}) copy-start(f32[2,64,512]{2,1,0:T(8,128)} %param.9) | copy-start | bytes 786436
  0.0 5.9 %copy-start.1 = (f32[2,64,512]{2,1,0:T(8,128)S(1)}, f32[2,64,512]{2,1,0:T(8,128)}, u32[]{:S(2)}) copy-start(f32[2,64,512]{2,1,0:T(8,128)} %param.10) | copy-start | bytes 786436
  2.2 15.2 %collective-permute-start = (f32[4,136,128]{2,1,0:T(8,128)}, f32[4,136,128]{2,1,0:T(8,128)S(1)}, u32[]{:S(2)}, u32[]{:S(2)}) collective-permute-start(f32[4,136,128]{2,1,0:T(8,128)} %get-tuple-element.34), channel_id=1, source_target_pairs={{0,1},{1,0},{2,3},{3,2},{4,5},{5,4},{6,7},{7,6},{8,9},{9,8},{10,11... | collective-permute-start | bytes 835592 | tf_op jit(solution)/shard_map/ppermute | solution.py:744
  5.2 12.2 %collective-permute-start.1 = (f32[4,136,128]{2,1,0:T(8,128)}, f32[4,136,128]{2,1,0:T(8,128)S(1)}, u32[]{:S(2)}, u32[]{:S(2)}) collective-permute-start(f32[4,136,128]{2,1,0:T(8,128)} %get-tuple-element.35), channel_id=1, source_target_pairs={{1,2},{2,1},{3,4},{4,3},{5,6},{6,5},{7,8},{8,7},{9,10},{10,9},{11,... | collective-permute-start | bytes 835592 | tf_op jit(solution)/shard_map/ppermute | solution.py:744
  5.9 11.5 %copy-start.3 = (s32[8,512]{1,0:T(8,128)S(1)}, s32[8,512]{1,0:T(8,128)}, u32[]{:S(2)}) copy-start(s32[8,512]{1,0:T(8,128)} %cells.1) | copy-start | bytes 49156
  6.0 11.5 %copy-start.4 = (s32[8]{0:T(128)S(1)}, s32[8]{0:T(128)}, u32[]{:S(2)}) copy-start(s32[8]{0:T(128)} %owner.3) | copy-start | bytes 100
  6.0 11.5 %copy-start.5 = (s32[8]{0:T(128)S(1)}, s32[8]{0:T(128)}, u32[]{:S(2)}) copy-start(s32[8]{0:T(128)} %order.3) | copy-start | bytes 100
  17.5 9.1 %copy-start.6 = (f32[8,512]{1,0:T(8,128)S(1)}, f32[8,512]{1,0:T(8,128)}, u32[]{:S(2)}) copy-start(f32[8,512]{1,0:T(8,128)} %param.15) | copy-start | bytes 49156
  17.5 10.6 %copy-start.2 = (f32[8,64,512]{2,1,0:T(8,128)S(1)}, f32[8,64,512]{2,1,0:T(8,128)}, u32[]{:S(2)}) copy-start(f32[8,64,512]{2,1,0:T(8,128)} %observed.1) | copy-start | bytes 3145732
  26.4 1.6 %collective-permute-start.2 = (f32[4,4,32,128]{3,2,1,0:T(8,128)S(1)}, f32[4,4,32,128]{3,2,1,0:T(8,128)S(1)}, u32[]{:S(2)}, u32[]{:S(2)}) collective-permute-start(f32[4,4,32,128]{3,2,1,0:T(8,128)S(1)} %get-tuple-element.42), channel_id=1, source_target_pairs={{0,16},{16,0},{1,17},{17,1},{2,18},{18,2},{3,19},{19,3},{4,20},{20... | collective-permute-start | bytes 786440 | tf_op jit(solution)/shard_map/ppermute | solution.py:749
  30.8 5.0 %collective-permute-start.3 = (f32[4,64,128]{2,1,0:T(8,128)S(1)}, f32[4,64,128]{2,1,0:T(8,128)S(1)}, u32[]{:S(2)}, u32[]{:S(2)}) collective-permute-start(f32[4,64,128]{2,1,0:T(8,128)S(1)} %gram.1), channel_id=1, source_target_pairs={{0,1},{1,0},{2,3},{3,2},{4,5},{5,4},{6,7},{7,6},{8,9},{9,8},{10,11... | collective-permute-start | bytes 393224 | tf_op jit(solution)/shard_map/ppermute | solution.py:756
  35.8 5.0 %collective-permute-start.4 = (f32[4,64,128]{2,1,0:T(8,128)S(1)}, f32[4,64,128]{2,1,0:T(8,128)S(1)}, u32[]{:S(2)}, u32[]{:S(2)}) collective-permute-start(f32[4,64,128]{2,1,0:T(8,128)S(1)} %add.12), channel_id=1, source_target_pairs={{0,2},{1,3},{2,0},{3,1},{4,6},{5,7},{6,4},{7,5},{8,10},{9,11},{10,... | collective-permute-start | bytes 393224 | tf_op jit(solution)/shard_map/ppermute | solution.py:756
  40.9 5.9 %collective-permute-start.5 = (f32[4,64,128]{2,1,0:T(8,128)S(1)}, f32[4,64,128]{2,1,0:T(8,128)S(1)}, u32[]{:S(2)}, u32[]{:S(2)}) collective-permute-start(f32[4,64,128]{2,1,0:T(8,128)S(1)} %add.13), channel_id=1, source_target_pairs={{0,4},{1,5},{2,6},{3,7},{4,0},{5,1},{6,2},{7,3},{8,12},{9,13},{10,... | collective-permute-start | bytes 393224 | tf_op jit(solution)/shard_map/ppermute | solution.py:756
  46.8 6.3 %collective-permute-start.6 = (f32[4,64,128]{2,1,0:T(8,128)S(1)}, f32[4,64,128]{2,1,0:T(8,128)S(1)}, u32[]{:S(2)}, u32[]{:S(2)}) collective-permute-start(f32[4,64,128]{2,1,0:T(8,128)S(1)} %add.14), channel_id=1, source_target_pairs={{0,8},{1,9},{2,10},{3,11},{4,12},{5,13},{6,14},{7,15},{8,0},{9,1},... | collective-permute-start | bytes 393224 | tf_op jit(solution)/shard_map/ppermute | solution.py:756
  53.2 1.4 %collective-permute-start.7 = (f32[4,64,128]{2,1,0:T(8,128)S(1)}, f32[4,64,128]{2,1,0:T(8,128)S(1)}, u32[]{:S(2)}, u32[]{:S(2)}) collective-permute-start(f32[4,64,128]{2,1,0:T(8,128)S(1)} %add.15.mine), channel_id=1, source_target_pairs={{0,16},{16,0},{1,17},{17,1},{2,18},{18,2},{3,19},{19,3},{4,20},{20... | collective-permute-start | bytes 393224 | tf_op jit(solution)/shard_map/ppermute | solution.py:766
  54.6 19.1 %collective-permute-start.8 = (f32[64,4,32,128]{3,2,1,0:T(8,128)S(1)}, f32[64,4,32,128]{3,2,1,0:T(8,128)S(1)}, u32[]{:S(2)}, u32[]{:S(2)}) collective-permute-start(f32[64,4,32,128]{3,2,1,0:T(8,128)S(1)} %get-tuple-element.61.own0), channel_id=1, source_target_pairs={{0,16},{16,0},{1,17},{17,1},{2,18},{18,2},{3,19},{19,3},{4,20},{20... | collective-permute-start | bytes 12582920 | tf_op jit(solution)/shard_map/ppermute | solution.py:768
  54.8 19.0 %collective-permute-start.9 = (f32[64,4,32,128]{3,2,1,0:T(8,128)S(1)}, f32[64,4,32,128]{3,2,1,0:T(8,128)S(1)}, u32[]{:S(2)}, u32[]{:S(2)}) collective-permute-start(f32[64,4,32,128]{3,2,1,0:T(8,128)S(1)} %forecast_members_3.1.own1), channel_id=1, source_target_pairs={{0,16},{16,0},{1,17},{17,1},{2,18},{18,2},{3,19},{19,3},{4,20},{20... | collective-permute-start | bytes 12582920 | tf_op jit(solution)/shard_map/ppermute | solution.py:769

commit v2 on v1

--- a/solution.py
+++ b/solution.py
@@ -12,7 +12,6 @@
 BF16 = jnp.bfloat16
 LANES = 128
 SUB = 8
-GATHER = 32
 AHEAD = 1
 PACK = 8
 
@@ -341,36 +340,48 @@
     nobs = cells.shape[1]
     tiles = full.reshape(rows * nct, members, LANES)
     lane = lax.broadcasted_iota(jnp.int32, (members, LANES), 1)
-    for position in range(order.shape[0]):
+
+    def gather_tile(batch, tile):
+        acc = jnp.zeros((members, LANES), F32)
+        for o in range(LANES):
+            cell = cells[batch, tile * LANES + o]
+            tile_at = lax.shift_right_logical(cell, LANES.bit_length() - 1)
+            moved = pltpu.roll(tiles[tile_at], (o - cell) & (LANES - 1), 1)
+            acc = jnp.where(lane == o, moved, acc)
+        return acc
+
+    def gather_batch(position, carry):
         batch = order[position]
         mine = owner[batch] == slab
         kept = lax.rem(position, 2) == member
-
-        def pick(tile, carry, batch=batch, mine=mine, kept=kept, position=position):
-            def some(group, acc):
-                for u in range(GATHER):
-                    o = group * GATHER + u
-                    cell = cells[batch, tile * LANES + o]
-                    tile_at = lax.shift_right_logical(cell, LANES.bit_length() - 1)
-                    moved = pltpu.roll(tiles[tile_at], (o - cell) & (LANES - 1), 1)
-                    acc = jnp.where(lane == o, moved, acc)
-                return acc
-
-            acc = lax.fori_loop(
-                0, jnp.where(mine, LANES // GATHER, 0), some, jnp.zeros((members, LANES), F32)
-            )
-
-            @pl.when(kept)
-            def _():
-                keep[position // 2, tile] = acc
-
-            @pl.when(jnp.logical_not(kept))
-            def _():
-                away[position // 2, tile] = acc
-
-            return carry
-
-        lax.fori_loop(0, nobs // LANES, pick, 0)
+        at = lax.div(position, 2)
+
+        for out, wanted in ((keep, kept), (away, jnp.logical_not(kept))):
+
+            @pl.when(jnp.logical_and(wanted, jnp.logical_not(mine)))
+            def _(out=out):
+                out[at] = jnp.zeros(out.shape[1:], F32)
+
+        @pl.when(mine)
+        def _():
+            def one(tile, carry):
+                values = gather_tile(batch, tile)
+
+                @pl.when(kept)
+                def _():
+                    keep[at, tile] = values
+
+                @pl.when(jnp.logical_not(kept))
+                def _():
+                    away[at, tile] = values
+
+                return carry
+
+            lax.fori_loop(0, nobs // LANES, one, 0)
+
+        return carry
+
+    lax.fori_loop(0, order.shape[0], gather_batch, 0)
 
 
 def forecast_edges(ids, cells, owner, order, flow5, nu5, before, after, full, held0, held1):

time: 83.9 us -> 84.8 us (1.011); the launches traced: 83.9 us -> 86.3 us
  starting transfers between devices: 4.63 us -> 21.9 us
  Pallas kernels: 60.9 us -> 51.9 us
  waiting for transfers between devices: 17.8 us -> 11.9 us
    ppermute x4, starting transfers between devices: 0.29 us -> 17.6 us  [body(): received = lax.ppermute(gh, 'space', [(i, i ^ bit) for i in range(space)])]
    pallas_call x1, Pallas kernels: 8.96 us -> 1.9 us  [forecast_edges(): pl.pallas_call(edge_kernel, out_shape=[*same, picks, picks], in_specs=[SM...]
    ppermute x4, waiting for transfers between devices: 12.4 us -> 6.53 us  [body(): received = lax.ppermute(gh, 'space', [(i, i ^ bit) for i in range(space)])]
    pallas_call x1, Pallas kernels: 2.69 us -> 0.79 us  [gram(): pl.pallas_call(gram_kernel, out_shape=jax.ShapeDtypeStruct((count, total,...]
  transfers between devices with their start and end apart: 10 -> 10, of which waited for: 7 -> 7; matrix products, arithmetic and copies ran while one was open for 0% -> 0% of each run, Pallas kernels for 44% -> 43%
where the time goes in v2:
time: 84.8 us; the launch traced here: 86.3 us
  Pallas kernels  51.9 us (61%)
  starting transfers between devices  21.9 us (26%)
  waiting for transfers between devices  11.9 us (14%)
    pallas_call x1, Pallas kernels, chain(): pl.pallas_call(chain_kernel, out_shape=jax.ShapeDtypeStruct((2 * size, 2...  18.6 us
    ppermute x4, starting transfers between devices, body(): received = lax.ppermute(gh, 'space', [(i, i ^ bit) for i in range(space)])  17.6 us
    pallas_call x1, Pallas kernels, apply(): pl.pallas_call(apply_kernel, out_shape=jax.ShapeDtypeStruct((size, 2, r8,...  9.96 us
    pallas_call x4, Pallas kernels, forecast_piece(): pl.pallas_call(functools.partial(piece_kernel, group), out_shape=jax.Shap...  9.59 us
    pallas_call x1, Pallas kernels, forecast_inner(): pl.pallas_call(inner_kernel, out_shape=[jax.ShapeDtypeStruct((r8 * SUB, n...  8.86 us
    ppermute x4, waiting for transfers between devices, body(): received = lax.ppermute(gh, 'space', [(i, i ^ bit) for i in range(space)])  6.53 us
    ppermute x2, starting transfers between devices, body(): lax.ppermute(x, 'space', pair)  3.68 us
    ppermute x2, waiting for transfers between devices, body(): lax.ppermute(x, 'space', pair)  2.52 us
  transfers between devices with their start and end apart: 10, of which 7 were waited for; matrix products, arithmetic and copies ran while one was open for 0% of the time, Pallas kernels for 43%

profile of v2, /device:TPU:0, one launch (start us, length us, event | category | flops | bytes accessed | tf_op | source)
XLA Modules:
  0.0 86.3 jit_solution(16714509408655821422)
XLA Ops:
  0.0 2.2 %pack_edges.1 = (f32[4,136,128]{2,1,0:T(8,128)}, f32[4,136,128]{2,1,0:T(8,128)}) custom-call(f32[32,2,8,4,8,128]{5,4,3,2,1,0:T(8,128)} %bitcast.28, f32[2,8,4,8,128]{4,3,2,1,0:T(8,128)} %bitcast.14, f32[2,8,4,8,128]{4,3,2,1,0:T(8,128)} %bitcast.21), custom_call_target="tpu_custom_call" | custom-call | tf_op jit(solution)/shard_map/pack_edges/pallas_call | solution.py:114
  2.2 3.0 %collective-permute-start = (f32[4,136,128]{2,1,0:T(8,128)}, f32[4,136,128]{2,1,0:T(8,128)S(1)}, u32[]{:S(2)}, u32[]{:S(2)}) collective-permute-start(f32[4,136,128]{2,1,0:T(8,128)} %get-tuple-element.34), channel_id=1, source_target_pairs={{0,1},{1,0},{2,3},{3,2},{4,5},{5,4},{6,7},{7,6},{8,9},{9,8},{10,11... | collective-permute-start | bytes 835592 | tf_op jit(solution)/shard_map/ppermute | solution.py:755
  5.2 0.7 collective-permute-start.1
  6.0 8.9 %forecast_inner.1 = (f32[64,4,32,128]{3,2,1,0:T(8,128)S(1)}, f32[4,4,8,10,8,128]{5,4,3,2,1,0:T(8,128)S(1)}, f32[4,4,8,10,8,128]{5,4,3,2,1,0:T(8,128)S(1)}) custom-call(f32[32,2,8,4,8,128]{5,4,3,2,1,0:T(8,128)} %bitcast.29, f32[2,8,4,8,128]{4,3,2,1,0:T(8,128)S(1)} %bitcast.15, f32[2,8,4,8,128]{4,3,2,1,0:T(8,128)S(1)} %bitcast.22), custom_call_target="tpu_custom_call" | custom-call | flops 41943040 | bytes 8388608 | tf_op jit(solution)/shard_map/forecast_inner/pallas_call | solution.py:286
  14.9 2.5 %collective-permute-done.before.first = f32[4,136,128]{2,1,0:T(8,128)S(1)} collective-permute-done((f32[4,136,128]{2,1,0:T(8,128)}, f32[4,136,128]{2,1,0:T(8,128)S(1)}, u32[]{:S(2)}, u32[]{:S(2)}) %collective-permute-start) | collective-permute-done | bytes 278560 | tf_op jit(solution)/shard_map/ppermute | solution.py:755
  17.5 1.9 %forecast_edges.1 = (f32[64,4,32,128]{3,2,1,0:T(8,128)S(1)}, f32[4,4,8,10,8,128]{5,4,3,2,1,0:T(8,128)S(1)}, f32[4,4,8,10,8,128]{5,4,3,2,1,0:T(8,128)S(1)}, f32[4...) custom-call(s32[2]{0:T(128)S(1)} %pad_add_fusion.ids, ...), custom_call_target="tpu_custom_call", output_to_operand_aliasing={{0}: (8, {}), {1}: (9, {}), {2}: (10, {})} | custom-call | flops 5242880 | bytes 1048576 | tf_op jit(solution)/shard_map/forecast_edges/pallas_call | solution.py:393
  19.5 1.5 %collective-permute-done.2.other = f32[4,4,32,128]{3,2,1,0:T(8,128)S(1)} collective-permute-done((f32[4,4,32,128]{3,2,1,0:T(8,128)S(1)}, f32[4,4,32,128]{3,2,1,0:T(8,128)S(1)}, u32[]{:S(2)}, u32[]{:S(2)}) %collective-permute-start.2) | collective-permute-done | bytes 262176 | tf_op jit(solution)/shard_map/ppermute | solution.py:760
  21.0 0.8 gram.1
  21.8 3.4 %collective-permute-start.3 = (f32[4,64,128]{2,1,0:T(8,128)S(1)}, f32[4,64,128]{2,1,0:T(8,128)S(1)}, u32[]{:S(2)}, u32[]{:S(2)}) collective-permute-start(f32[4,64,128]{2,1,0:T(8,128)S(1)} %gram.1), channel_id=1, source_target_pairs={{0,1},{1,0},{2,3},{3,2},{4,5},{5,4},{6,7},{7,6},{8,9},{9,8},{10,11... | collective-permute-start | bytes 393224 | tf_op jit(solution)/shard_map/ppermute | solution.py:767
  25.2 2.4 %forecast_members_0.1.rest_0_ = f32[64,4,32,128]{3,2,1,0:T(8,128)S(1)} custom-call(s32[2]{0:T(128)S(1)} %pad_add_fusion.ids, f32[2,8,4,8,128]{4,3,2,1,0:T(8,128)S(1)} %bitcast.17, f32[2,8,4,8,128]{4,3,2,1,0:T(8,128)S(1)} %bitcast.24, f32[4,136,128]{2,1,0:T(8,128)S(1)} %collective-permute-done.before.first, ...), custom_call_target="tpu_custom_call" | custom-call | flops 10485760 | bytes 2097152 | tf_op jit(solution)/shard_map/forecast_members_0/pallas_call | solution.py:423
  27.6 1.4 %collective-permute-done.3 = f32[4,64,128]{2,1,0:T(8,128)S(1)} collective-permute-done((f32[4,64,128]{2,1,0:T(8,128)S(1)}, f32[4,64,128]{2,1,0:T(8,128)S(1)}, u32[]{:S(2)}, u32[]{:S(2)}) %collective-permute-start.3) | collective-permute-done | bytes 131104 | tf_op jit(solution)/shard_map/ppermute | solution.py:767
  29.0 0.6 collective-permute-start.4
  29.6 2.4 %forecast_members_1.1.rest_0_ = f32[64,4,32,128]{3,2,1,0:T(8,128)S(1)} custom-call(s32[2]{0:T(128)S(1)} %pad_add_fusion.ids, f32[2,8,4,8,128]{4,3,2,1,0:T(8,128)S(1)} %bitcast.18, f32[2,8,4,8,128]{4,3,2,1,0:T(8,128)S(1)} %bitcast.25, f32[4,136,128]{2,1,0:T(8,128)S(1)} %collective-permute-done.before.first, ...), custom_call_target="tpu_custom_call", output_to_operand_aliasing={{}: (6, {})} | custom-call | flops 10485760 | bytes 2097152 | tf_op jit(solution)/shard_map/forecast_members_1/pallas_call | solution.py:423
  32.0 2.1 %collective-permute-done.4 = f32[4,64,128]{2,1,0:T(8,128)S(1)} collective-permute-done((f32[4,64,128]{2,1,0:T(8,128)S(1)}, f32[4,64,128]{2,1,0:T(8,128)S(1)}, u32[]{:S(2)}, u32[]{:S(2)}) %collective-permute-start.4) | collective-permute-done | bytes 131104 | tf_op jit(solution)/shard_map/ppermute | solution.py:767
  34.1 4.4 %collective-permute-start.5 = (f32[4,64,128]{2,1,0:T(8,128)S(1)}, f32[4,64,128]{2,1,0:T(8,128)S(1)}, u32[]{:S(2)}, u32[]{:S(2)}) collective-permute-start(f32[4,64,128]{2,1,0:T(8,128)S(1)} %add.13), channel_id=1, source_target_pairs={{0,4},{1,5},{2,6},{3,7},{4,0},{5,1},{6,2},{7,3},{8,12},{9,13},{10,... | collective-permute-start | bytes 393224 | tf_op jit(solution)/shard_map/ppermute | solution.py:767
  38.6 2.4 %forecast_members_2.1.rest_0_ = f32[64,4,32,128]{3,2,1,0:T(8,128)S(1)} custom-call(s32[2]{0:T(128)S(1)} %pad_add_fusion.ids, f32[2,8,4,8,128]{4,3,2,1,0:T(8,128)S(1)} %bitcast.19, f32[2,8,4,8,128]{4,3,2,1,0:T(8,128)S(1)} %bitcast.26, f32[4,136,128]{2,1,0:T(8,128)S(1)} %collective-permute-done.before.first, ...), custom_call_target="tpu_custom_call", output_to_operand_aliasing={{}: (6, {})} | custom-call | flops 10485760 | bytes 2097152 | tf_op jit(solution)/shard_map/forecast_members_2/pallas_call | solution.py:423
  41.0 0.5 collective-permute-done.5
  41.5 9.2 %collective-permute-start.6 = (f32[4,64,128]{2,1,0:T(8,128)S(1)}, f32[4,64,128]{2,1,0:T(8,128)S(1)}, u32[]{:S(2)}, u32[]{:S(2)}) collective-permute-start(f32[4,64,128]{2,1,0:T(8,128)S(1)} %add.14), channel_id=1, source_target_pairs={{0,8},{1,9},{2,10},{3,11},{4,12},{5,13},{6,14},{7,15},{8,0},{9,1},... | collective-permute-start | bytes 393224 | tf_op jit(solution)/shard_map/ppermute | solution.py:767
  50.7 2.4 %forecast_members_3.1.own1 = f32[64,4,32,128]{3,2,1,0:T(8,128)S(1)} custom-call(s32[2]{0:T(128)S(1)} %pad_add_fusion.ids, f32[2,8,4,8,128]{4,3,2,1,0:T(8,128)S(1)} %bitcast.20, f32[2,8,4,8,128]{4,3,2,1,0:T(8,128)S(1)} %bitcast.27, f32[4,136,128]{2,1,0:T(8,128)S(1)} %collective-permute-done.before.first, ...), custom_call_target="tpu_custom_call", output_to_operand_aliasing={{}: (6, {})} | custom-call | flops 10485760 | bytes 2097152 | tf_op jit(solution)/shard_map/forecast_members_3/pallas_call | solution.py:423
  53.1 2.5 %collective-permute-done.6 = f32[4,64,128]{2,1,0:T(8,128)S(1)} collective-permute-done((f32[4,64,128]{2,1,0:T(8,128)S(1)}, f32[4,64,128]{2,1,0:T(8,128)S(1)}, u32[]{:S(2)}, u32[]{:S(2)}) %collective-permute-start.6) | collective-permute-done | bytes 131104 | tf_op jit(solution)/shard_map/ppermute | solution.py:767
  55.7 1.3 %collective-permute-done.7.other = f32[4,64,128]{2,1,0:T(8,128)S(1)} collective-permute-done((f32[4,64,128]{2,1,0:T(8,128)S(1)}, f32[4,64,128]{2,1,0:T(8,128)S(1)}, u32[]{:S(2)}, u32[]{:S(2)}) %collective-permute-start.7) | collective-permute-done | bytes 131104 | tf_op jit(solution)/shard_map/ppermute | solution.py:777
  57.2 0.4 collective-permute-start.9
  57.5 18.6 %chain.1.w_ref = f32[128,128]{1,0:T(8,128)S(1)} custom-call(s32[2]{0:T(128)S(1)} %pad_add_fusion.ids, f32[4,64,128]{2,1,0:T(8,128)S(1)} %add.15.mine, f32[4,64,128]{2,1,0:T(8,128)S(1)} %collective-permute-done.7.other), custom_call_target="tpu_custom_call" | custom-call | tf_op jit(solution)/shard_map/chain/pallas_call | solution.py:668
  76.2 10.0 %apply.1 = f32[64,2,8,2,8,128]{5,4,3,2,1,0:T(8,128)} custom-call(s32[2]{0:T(128)S(1)} %pad_add_fusion.ids, f32[128,128]{1,0:T(8,128)S(1)} %chain.1.w_ref, f32[64,4,32,128]{3,2,1,0:T(8,128)S(1)} %get-tuple-element.61.own0, f32[64,4,32,128]{3,2,1,0:T(8,128)S(1)} %collective-permute-done.8.other0, f32[64,4,32,128]{3,2,1,0:T(8,128)S(1)} %forecast_members_3.1.own1, ...), custom_call_target="tpu_custom_call" | custom-call | tf_op jit(solution)/shard_map/apply/pallas_call | solution.py:729
  (26 shorter events, 0.5 us)
Async XLA Ops:
  0.0 5.9 %copy-start = (f32[2,64,512]{2,1,0:T(8,128)S(1)}, f32[2,64,512]{2,1,0:T(8,128)}, u32[]{:S(2)}) copy-start(f32[2,64,512]{2,1,0:T(8,128)} %param.9) | copy-start | bytes 786436
  0.0 5.9 %copy-start.1 = (f32[2,64,512]{2,1,0:T(8,128)S(1)}, f32[2,64,512]{2,1,0:T(8,128)}, u32[]{:S(2)}) copy-start(f32[2,64,512]{2,1,0:T(8,128)} %param.10) | copy-start | bytes 786436
  2.2 15.2 %collective-permute-start = (f32[4,136,128]{2,1,0:T(8,128)}, f32[4,136,128]{2,1,0:T(8,128)S(1)}, u32[]{:S(2)}, u32[]{:S(2)}) collective-permute-start(f32[4,136,128]{2,1,0:T(8,128)} %get-tuple-element.34), channel_id=1, source_target_pairs={{0,1},{1,0},{2,3},{3,2},{4,5},{5,4},{6,7},{7,6},{8,9},{9,8},{10,11... | collective-permute-start | bytes 835592 | tf_op jit(solution)/shard_map/ppermute | solution.py:755
  5.2 12.2 %collective-permute-start.1 = (f32[4,136,128]{2,1,0:T(8,128)}, f32[4,136,128]{2,1,0:T(8,128)S(1)}, u32[]{:S(2)}, u32[]{:S(2)}) collective-permute-start(f32[4,136,128]{2,1,0:T(8,128)} %get-tuple-element.35), channel_id=1, source_target_pairs={{1,2},{2,1},{3,4},{4,3},{5,6},{6,5},{7,8},{8,7},{9,10},{10,9},{11,... | collective-permute-start | bytes 835592 | tf_op jit(solution)/shard_map/ppermute | solution.py:755
  5.9 11.5 %copy-start.3 = (s32[8,512]{1,0:T(8,128)S(1)}, s32[8,512]{1,0:T(8,128)}, u32[]{:S(2)}) copy-start(s32[8,512]{1,0:T(8,128)} %cells.1) | copy-start | bytes 49156
  6.0 11.5 %copy-start.4 = (s32[8]{0:T(128)S(1)}, s32[8]{0:T(128)}, u32[]{:S(2)}) copy-start(s32[8]{0:T(128)} %owner.3) | copy-start | bytes 100
  6.0 11.5 %copy-start.5 = (s32[8]{0:T(128)S(1)}, s32[8]{0:T(128)}, u32[]{:S(2)}) copy-start(s32[8]{0:T(128)} %order.3) | copy-start | bytes 100
  17.5 2.0 %copy-start.6 = (f32[8,512]{1,0:T(8,128)S(1)}, f32[8,512]{1,0:T(8,128)}, u32[]{:S(2)}) copy-start(f32[8,512]{1,0:T(8,128)} %param.15) | copy-start | bytes 49156
  17.5 3.5 %copy-start.2 = (f32[8,64,512]{2,1,0:T(8,128)S(1)}, f32[8,64,512]{2,1,0:T(8,128)}, u32[]{:S(2)}) copy-start(f32[8,64,512]{2,1,0:T(8,128)} %observed.1) | copy-start | bytes 3145732
  19.4 1.6 %collective-permute-start.2 = (f32[4,4,32,128]{3,2,1,0:T(8,128)S(1)}, f32[4,4,32,128]{3,2,1,0:T(8,128)S(1)}, u32[]{:S(2)}, u32[]{:S(2)}) collective-permute-start(f32[4,4,32,128]{3,2,1,0:T(8,128)S(1)} %get-tuple-element.42), channel_id=1, source_target_pairs={{0,16},{16,0},{1,17},{17,1},{2,18},{18,2},{3,19},{19,3},{4,20},{20... | collective-permute-start | bytes 786440 | tf_op jit(solution)/shard_map/ppermute | solution.py:760
  21.8 7.2 %collective-permute-start.3 = (f32[4,64,128]{2,1,0:T(8,128)S(1)}, f32[4,64,128]{2,1,0:T(8,128)S(1)}, u32[]{:S(2)}, u32[]{:S(2)}) collective-permute-start(f32[4,64,128]{2,1,0:T(8,128)S(1)} %gram.1), channel_id=1, source_target_pairs={{0,1},{1,0},{2,3},{3,2},{4,5},{5,4},{6,7},{7,6},{8,9},{9,8},{10,11... | collective-permute-start | bytes 393224 | tf_op jit(solution)/shard_map/ppermute | solution.py:767
  29.0 5.1 %collective-permute-start.4 = (f32[4,64,128]{2,1,0:T(8,128)S(1)}, f32[4,64,128]{2,1,0:T(8,128)S(1)}, u32[]{:S(2)}, u32[]{:S(2)}) collective-permute-start(f32[4,64,128]{2,1,0:T(8,128)S(1)} %add.12), channel_id=1, source_target_pairs={{0,2},{1,3},{2,0},{3,1},{4,6},{5,7},{6,4},{7,5},{8,10},{9,11},{10,... | collective-permute-start | bytes 393224 | tf_op jit(solution)/shard_map/ppermute | solution.py:767
  34.1 7.4 %collective-permute-start.5 = (f32[4,64,128]{2,1,0:T(8,128)S(1)}, f32[4,64,128]{2,1,0:T(8,128)S(1)}, u32[]{:S(2)}, u32[]{:S(2)}) collective-permute-start(f32[4,64,128]{2,1,0:T(8,128)S(1)} %add.13), channel_id=1, source_target_pairs={{0,4},{1,5},{2,6},{3,7},{4,0},{5,1},{6,2},{7,3},{8,12},{9,13},{10,... | collective-permute-start | bytes 393224 | tf_op jit(solution)/shard_map/ppermute | solution.py:767
  41.5 14.1 %collective-permute-start.6 = (f32[4,64,128]{2,1,0:T(8,128)S(1)}, f32[4,64,128]{2,1,0:T(8,128)S(1)}, u32[]{:S(2)}, u32[]{:S(2)}) collective-permute-start(f32[4,64,128]{2,1,0:T(8,128)S(1)} %add.14), channel_id=1, source_target_pairs={{0,8},{1,9},{2,10},{3,11},{4,12},{5,13},{6,14},{7,15},{8,0},{9,1},... | collective-permute-start | bytes 393224 | tf_op jit(solution)/shard_map/ppermute | solution.py:767
  55.6 1.4 %collective-permute-start.7 = (f32[4,64,128]{2,1,0:T(8,128)S(1)}, f32[4,64,128]{2,1,0:T(8,128)S(1)}, u32[]{:S(2)}, u32[]{:S(2)}) collective-permute-start(f32[4,64,128]{2,1,0:T(8,128)S(1)} %add.15.mine), channel_id=1, source_target_pairs={{0,16},{16,0},{1,17},{17,1},{2,18},{18,2},{3,19},{19,3},{4,20},{20... | collective-permute-start | bytes 393224 | tf_op jit(solution)/shard_map/ppermute | solution.py:777
  57.0 19.1 %collective-permute-start.8 = (f32[64,4,32,128]{3,2,1,0:T(8,128)S(1)}, f32[64,4,32,128]{3,2,1,0:T(8,128)S(1)}, u32[]{:S(2)}, u32[]{:S(2)}) collective-permute-start(f32[64,4,32,128]{3,2,1,0:T(8,128)S(1)} %get-tuple-element.61.own0), channel_id=1, source_target_pairs={{0,16},{16,0},{1,17},{17,1},{2,18},{18,2},{3,19},{19,3},{4,20},{20... | collective-permute-start | bytes 12582920 | tf_op jit(solution)/shard_map/ppermute | solution.py:779
  57.2 19.0 %collective-permute-start.9 = (f32[64,4,32,128]{3,2,1,0:T(8,128)S(1)}, f32[64,4,32,128]{3,2,1,0:T(8,128)S(1)}, u32[]{:S(2)}, u32[]{:S(2)}) collective-permute-start(f32[64,4,32,128]{3,2,1,0:T(8,128)S(1)} %forecast_members_3.1.own1), channel_id=1, source_target_pairs={{0,16},{16,0},{1,17},{17,1},{2,18},{18,2},{3,19},{19,3},{4,20},{20... | collective-permute-start | bytes 12582920 | tf_op jit(solution)/shard_map/ppermute | solution.py:780
